TPU v7x, 256 devices: a whole 4x4x8 slice. The times are simulated.
256 devices in a mesh: ta: 4 (over z_lo), sa: 64 (over x, y, z_hi, core).
Axes of the slice: x: 4, y: 4, z: 8 (z_hi: 2, z_lo: 4; z = z_hi * 4 + z_lo), core: 2. Of those that a mesh axis runs over, the one named last changes fastest.
Arguments:
- video_q: bfloat16 [4, 64, 384, 1536], P('ta', 'sa'), may hold values from -8 to 8
- video_k: bfloat16 [4, 64, 384, 1536], P('ta', 'sa'), may hold values from -8 to 8
- video_v: bfloat16 [4, 64, 384, 1536], P('ta', 'sa'), may hold values from -6 to 6
- text_q: bfloat16 [256, 1536], P(('ta', 'sa')), may hold values from -8 to 8
- text_k: bfloat16 [256, 1536], P(('ta', 'sa')), may hold values from -8 to 8
- text_v: bfloat16 [256, 1536], P(('ta', 'sa')), may hold values from -6 to 6
- q_gain: float32 [128], replicated, may hold values from 1 to 5.5
- k_gain: float32 [128], replicated, may hold values from 1 to 5.5
- text_len: int32 [1], replicated, may hold values from 64 to 256
- window: int32 [12, 3], replicated, may hold values from 1 to 3, as said below
Outputs:
- video_out: bfloat16 [4, 64, 384, 1536], P('ta', 'sa')
- text_out: bfloat16 [256, 1536], P(('ta', 'sa'))
Inputs may be any that keep to these rules, and one draw needn't show every extreme that they name: Each head's window is 1 or 3 tiles along each of time, spatial rows and spatial columns; exactly 2 heads have each of the windows (3,3,3), (1,3,3), (3,1,3), (3,3,1), (1,1,3) and (1,3,1).
All inputs are finite; a program needn't handle non-finite values.
Results may differ from a plain program's by a relative error of at most 0.018.
The roundings to bfloat16 on the way count: a program that leaves them out, or rounds other values in their place, can miss the bound.
Values may be sent and summed in bfloat16 or wider, within the bound.
A program may use at most 128 MiB of HBM per device.

v0:
```python
import math

import jax
import jax.numpy as jnp
from jax import lax
from jax.sharding import PartitionSpec as P

SW = 8


EPSILON = 1e-06
WINDOW_SHAPES = ((1, 1, 1), (0, 1, 1), (1, 0, 1), (1, 1, 0), (0, 0, 1), (0, 1, 0))


def with_halo(block, sides, width):
    for axis, dim in sides:
        count = lax.axis_size(axis)
        forward = [(i, i + 1) for i in range(count - 1)]
        backward = [(target, source) for source, target in forward]
        low = lax.ppermute(
            lax.slice_in_dim(block, block.shape[dim] - width, None, axis=dim), axis, forward
        )
        high = lax.ppermute(lax.slice_in_dim(block, 0, width, axis=dim), axis, backward)
        block = jnp.concatenate([low, block, high], axis=dim)
    return block


def shifted(value, axis, steps):
    count = lax.axis_size(axis)
    initial, last = (max(0, -steps), min(count, count - steps))
    return lax.ppermute(value, axis, [(source, source + steps) for source in range(initial, last)])


def normalize(values, gain_vector):
    per_head = gain_vector.shape[0]
    shaped = values.astype(jnp.float32).reshape(
        values.shape[:-1] + (values.shape[-1] // per_head, per_head)
    )
    spread = jnp.sqrt(jnp.mean(shaped * shaped, axis=-1, keepdims=True) + EPSILON)
    return (shaped / spread * gain_vector).astype(jnp.bfloat16)


def neighbours(combined, dimension):
    tile_count = combined.shape[1]
    if dimension == 0:
        extended = with_halo(combined, (("ta", 1),), 1)
        return (extended[:, :tile_count], extended[:, 2:])
    stride = SW if dimension == 1 else 1
    arrived = [shifted(combined, "sa", amount) for amount in (stride, -stride)]
    return (arrived[0], arrived[1])


def stepped(offset, dimension, delta):
    return tuple(
        (value + delta if place == dimension else value for place, value in enumerate(offset))
    )


def widen(slabs, offsets, dimension):
    taking = [number for number, flags in enumerate(WINDOW_SHAPES) if flags[dimension] == 1]
    flattened = []
    for number in taking:
        layout = slabs[number].shape
        flattened.append(slabs[number].reshape(layout[:3] + (layout[3] * layout[4], layout[5])))
    combined = jnp.concatenate(flattened, axis=3)
    lower, upper = neighbours(combined, dimension)
    new_slabs = list(slabs)
    new_offsets = list(offsets)
    position = 0
    for number in taking:
        layout = slabs[number].shape
        amount = layout[3] * layout[4]
        lower_part = lower[:, :, :, position : position + amount].reshape(layout)
        upper_part = upper[:, :, :, position : position + amount].reshape(layout)
        new_slabs[number] = jnp.concatenate([lower_part, slabs[number], upper_part], axis=3)
        old = offsets[number]
        new_offsets[number] = (
            [stepped(item, dimension, -1) for item in old]
            + list(old)
            + [stepped(item, dimension, 1) for item in old]
        )
        position = position + amount
    return (new_slabs, new_offsets)


def inside_grid(offset_list, global_time, time_total, row_index, row_total, column_index):
    flags = []
    for offset in offset_list:
        moved_time = global_time + offset[0]
        moved_row = row_index + offset[1]
        moved_column = column_index + offset[2]
        valid = (moved_time >= 0) & (moved_time < time_total)
        valid = (
            valid
            & (moved_row >= 0)
            & (moved_row < row_total)
            & (moved_column >= 0)
            & (moved_column < SW)
        )
        flags.append(valid)
    return jnp.stack(flags, axis=1)


def local(video_q, video_k, video_v, text_q, text_k, text_v, q_gain, k_gain, text_len, window):
    head_count = window.shape[0]
    per_head = q_gain.shape[0]
    tile_count = video_q.shape[0]
    tile_tokens = video_q.shape[2]
    own_rows = text_q.shape[0]
    per_shape = head_count // 6
    score_scale = 1.0 / math.sqrt(per_head)
    queries = normalize(video_q[:, 0], q_gain)
    key_tiles = normalize(video_k[:, 0], k_gain)
    value_tiles = video_v[:, 0].reshape(key_tiles.shape)
    text_parts = (
        normalize(text_q, q_gain),
        normalize(text_k, k_gain),
        text_v.reshape(own_rows, head_count, per_head),
    )
    text_queries, text_keys, text_values = (
        lax.all_gather(text_parts[0], ("ta", "sa"), axis=0, tiled=True),
        lax.all_gather(text_parts[1], ("ta", "sa"), axis=0, tiled=True),
        lax.all_gather(text_parts[2], ("ta", "sa"), axis=0, tiled=True),
    )
    text_count = text_keys.shape[0]
    text_ok = jnp.arange(text_count, dtype=jnp.int32) < text_len[0]
    widened = (window == 3).astype(jnp.int32)
    shape_code = widened[:, 0] * 4 + widened[:, 1] * 2 + widened[:, 2]
    members = []
    for flags in WINDOW_SHAPES:
        wanted = flags[0] * 4 + flags[1] * 2 + flags[2]
        members.append(
            jnp.argsort((shape_code != wanted).astype(jnp.int32), stable=True)[:per_shape]
        )
    key_value = jnp.stack((key_tiles, value_tiles))
    slabs = [jnp.take(key_value, chosen, axis=3)[:, :, :, None] for chosen in members]
    offsets = [[(0, 0, 0)] for flags in WINDOW_SHAPES]
    section_order = (2, 1, 0)
    for dimension in section_order:
        slabs, offsets = widen(slabs, offsets, dimension)
    global_time = lax.axis_index("ta") * tile_count + jnp.arange(tile_count, dtype=jnp.int32)
    time_total = tile_count * lax.axis_size("ta")
    space_index = lax.axis_index("sa")
    row_index = space_index // SW
    column_index = space_index % SW
    row_total = lax.axis_size("sa") // SW
    rows_block = 128
    block_count = tile_tokens // rows_block
    items = tile_count * per_shape

    def attend_item(inputs):
        item_queries, item_keys, item_values, item_mask, item_text_keys, item_text_values = inputs

        def attend_block(block_queries):
            video_scores = (
                jnp.einsum(
                    "qd,kd->qk", block_queries, item_keys, preferred_element_type=jnp.float32
                )
                * score_scale
            )
            video_scores = jnp.where(item_mask[None, :], video_scores, -jnp.inf)
            text_scores = (
                jnp.einsum(
                    "qd,kd->qk", block_queries, item_text_keys, preferred_element_type=jnp.float32
                )
                * score_scale
            )
            text_scores = jnp.where(text_ok[None, :], text_scores, -jnp.inf)
            highest = jnp.maximum(jnp.max(video_scores, axis=-1), jnp.max(text_scores, axis=-1))
            video_weights = jnp.exp(video_scores - highest[:, None])
            text_weights = jnp.exp(text_scores - highest[:, None])
            totals = jnp.sum(video_weights, axis=-1) + jnp.sum(text_weights, axis=-1)
            summed = jnp.einsum(
                "qk,kd->qd",
                video_weights.astype(jnp.bfloat16),
                item_values,
                preferred_element_type=jnp.float32,
            )
            summed = summed + jnp.einsum(
                "qk,kd->qd",
                text_weights.astype(jnp.bfloat16),
                item_text_values,
                preferred_element_type=jnp.float32,
            )
            return (summed / totals[:, None]).astype(jnp.bfloat16)

        return lax.map(attend_block, item_queries)

    outputs = []
    for number in range(6):
        chosen = members[number]
        slab = slabs[number]
        span = slab.shape[3]
        key_rows = jnp.transpose(slab, (0, 1, 4, 3, 2, 5)).reshape(
            2, items, span * tile_tokens, per_head
        )
        tile_mask = jnp.repeat(
            inside_grid(
                offsets[number], global_time, time_total, row_index, row_total, column_index
            ),
            tile_tokens,
            axis=1,
        )
        item_mask = jnp.broadcast_to(
            tile_mask[:, None, :], (tile_count, per_shape, span * tile_tokens)
        ).reshape(items, span * tile_tokens)
        class_queries = jnp.transpose(jnp.take(queries, chosen, axis=2), (0, 2, 1, 3)).reshape(
            items, block_count, rows_block, per_head
        )
        class_text_keys = jnp.transpose(jnp.take(text_keys, chosen, axis=1), (1, 0, 2))
        class_text_values = jnp.transpose(jnp.take(text_values, chosen, axis=1), (1, 0, 2))
        item_text_keys = class_text_keys[None].reshape(items, text_count, per_head)
        item_text_values = class_text_values[None].reshape(items, text_count, per_head)
        result = lax.map(
            attend_item,
            (class_queries, key_rows[0], key_rows[1], item_mask, item_text_keys, item_text_values),
        )
        outputs.append(
            jnp.transpose(
                result.reshape(tile_count, per_shape, tile_tokens, per_head), (0, 2, 1, 3)
            )
        )
    ordered = jnp.concatenate(outputs, axis=2)
    placement = jnp.argsort(jnp.concatenate(members))
    video_out = jnp.take(ordered, placement, axis=2).reshape(
        tile_count, 1, tile_tokens, head_count * per_head
    )
    tile_scores = (
        jnp.einsum("qhd,jkhd->jhqk", text_queries, key_tiles, preferred_element_type=jnp.float32)
        * score_scale
    )
    tile_peaks = jnp.max(tile_scores, axis=-1)
    tile_weights = jnp.exp(tile_scores - tile_peaks[..., None])
    tile_totals = jnp.sum(tile_weights, axis=-1)
    tile_sums = jnp.einsum(
        "jhqk,jkhd->jhqd",
        tile_weights.astype(jnp.bfloat16),
        value_tiles,
        preferred_element_type=jnp.float32,
    )
    self_scores = (
        jnp.einsum("qhd,khd->hqk", text_queries, text_keys, preferred_element_type=jnp.float32)
        * score_scale
    )
    self_scores = jnp.where(text_ok[None, None, :], self_scores, -jnp.inf)
    self_peaks = jnp.max(self_scores, axis=-1)
    self_weights = jnp.exp(self_scores - self_peaks[..., None])
    self_totals = jnp.sum(self_weights, axis=-1)
    self_sums = jnp.einsum(
        "hqk,khd->hqd",
        self_weights.astype(jnp.bfloat16),
        text_values,
        preferred_element_type=jnp.float32,
    )
    is_first = lax.axis_index(("ta", "sa")) == 0
    self_peaks = jnp.where(is_first, self_peaks, -1e30)
    joint_peak = jnp.maximum(jnp.max(tile_peaks, axis=0), self_peaks)
    tile_factor = jnp.exp(tile_peaks - joint_peak[None])
    self_factor = jnp.exp(self_peaks - joint_peak)
    weight_total = jnp.sum(tile_totals * tile_factor, axis=0) + self_totals * self_factor
    summed = (
        jnp.sum(tile_sums * tile_factor[..., None], axis=0) + self_sums * self_factor[..., None]
    )
    peak_value = lax.pmax(joint_peak, ("ta", "sa"))
    factor = jnp.exp(joint_peak - peak_value)
    scaled_sums = summed * factor[..., None]
    scaled_totals = weight_total * factor
    whole_sums, whole_totals = lax.psum((scaled_sums, scaled_totals), ("ta", "sa"))
    first_row = lax.axis_index(("ta", "sa")) * own_rows
    share_sums = lax.dynamic_slice_in_dim(whole_sums, first_row, own_rows, 1)
    share_totals = lax.dynamic_slice_in_dim(whole_totals, first_row, own_rows, 1)
    text_result = share_sums / share_totals[..., None]
    text_out = (
        jnp.transpose(text_result, (1, 0, 2))
        .reshape(own_rows, head_count * per_head)
        .astype(jnp.bfloat16)
    )
    return (video_out, text_out)


def solution(mesh):
    return jax.shard_map(
        local,
        mesh=mesh,
        in_specs=(
            P("ta", "sa", None, None),
            P("ta", "sa", None, None),
            P("ta", "sa", None, None),
            P(("ta", "sa"), None),
            P(("ta", "sa"), None),
            P(("ta", "sa"), None),
            P(),
            P(),
            P(),
            P(),
        ),
        out_specs=(P("ta", "sa", None, None), P(("ta", "sa"), None)),
        check_vma=False,
    )
```

profile of v0, /device:TPU:36, one launch (start us, length us, event | category | flops | bytes accessed | tf_op | source)
XLA Modules:
  0.0 2127.5 jit_solution(13645116001768265986)
XLA Ops:
  36.8 10.0 collective-permute-start.1
  50.5 472.8 %all_gather.11 = bf16[256,12,128]{2,1,0:T(8,128)(2,1)} all-gather(bf16[1,12,128]{2,1,0:T(8,128)(2,1)S(1)} %fusion.166), channel_id=1, replica_groups=mesh['ta'=4,'sa'=64] {'ta','sa'}, dimensions={0}, use_global_device_ids=true | all-gather | bytes 789504 | tf_op jit(solution)/shard_map/all_gather | solution.py:121
  523.3 390.7 %all_gather.9 = bf16[256,12,128]{2,1,0:T(8,128)(2,1)S(1)} all-gather(bf16[1,12,128]{2,1,0:T(8,128)(2,1)S(1)} %fusion.169), channel_id=1, replica_groups=mesh['ta'=4,'sa'=64] {'ta','sa'}, dimensions={0}, use_global_device_ids=true | all-gather | bytes 789504 | tf_op jit(solution)/shard_map/all_gather | solution.py:122
  915.3 404.1 %all_gather.10 = bf16[256,12,128]{2,1,0:T(8,128)(2,1)S(1)} all-gather(bf16[1,12,128]{2,1,0:T(8,128)(2,1)S(1)} %bitcast.707), channel_id=1, replica_groups=mesh['ta'=4,'sa'=64] {'ta','sa'}, dimensions={0}, use_global_device_ids=true | all-gather | bytes 789504 | tf_op jit(solution)/shard_map/all_gather | solution.py:123
  1326.9 93.1 %pmax.7 = f32[12,256]{1,0:T(8,128)} all-reduce(f32[12,256]{1,0:T(8,128)} %select_maximum_fusion), channel_id=1, replica_groups=mesh['ta'=4,'sa'=64] {'ta','sa'}, use_global_device_ids=true, to_apply=%region_61.65 | all-reduce | flops 3072 | bytes 24576 | tf_op jit(solution)/shard_map/pmax | solution.py:264
  1483.6 73.6 %psum.15 = f32[12,256]{1,0:T(8,128)S(1)} all-reduce(f32[12,256]{1,0:T(8,128)S(1)} %get-tuple-element.999), channel_id=1, replica_groups=mesh['ta'=4,'sa'=64] {'ta','sa'}, use_global_device_ids=true, to_apply=%region_65.69 | all-reduce | flops 3072 | bytes 24576 | tf_op jit(solution)/shard_map/psum | solution.py:268
  1560.0 122.6 %all-reduce.2.cloned.1.call-done = f32[12,256,128]{2,1,0:T(8,128)} async-done(((f32[12,256,128]{2,1,0:T(8,128)}), f32[12,256,128]{2,1,0:T(8,128)}) %all-reduce.2.cloned.1.call-update) | async-done | bytes 1572880 | tf_op jit(solution)/shard_map/psum | solution.py:268
  1701.3 22.9 %while.141 = (s32[]{:T(128)}, bf16[2,3,128,128]{3,2,1,0:T(8,128)(2,1)}, bf16[2,3,128,128]{3,2,1,0:T(8,128)(2,1)}, bf16[2,1152,128]{2,1,0:T(8,128)(2,1)S(1)}, pre...) while((s32[]{:T(128)}, ...), condition=%wide.region_49.53_spmd.clone, body=%wide.region_42.52_spmd.clone.sunk | while | flops 93585408 | bytes 5223298 | solution.py:214
  1704.6 6.7 while.148
  1716.0 6.7 while.148
  1725.5 108.2 %collective-permute-done.3 = bf16[2,1,384,16,128]{4,2,0,3,1:T(8,128)(2,1)} collective-permute-done((bf16[2,1,384,16,128]{4,2,0,3,1:T(8,128)(2,1)}, bf16[2,1,384,16,128]{4,2,0,3,1:T(8,128)(2,1)}, u32[]{:S(2)}, u32[]{:S(2)}) %collective-permute-start.3) | collective-permute-done | bytes 3145760 | tf_op jit(solution)/shard_map/ppermute | solution.py:31
  1858.9 22.0 %while.135 = (s32[]{:T(128)}, bf16[2,3,128,128]{3,2,1,0:T(8,128)(2,1)}, bf16[2,3,128,128]{3,2,1,0:T(8,128)(2,1)}, bf16[2,3456,128]{2,1,0:T(8,128)(2,1)}, pred[2,...) while((s32[]{:T(128)}, ...), condition=%wide.region_25.29_spmd.clone, body=%wide.region_18.28_spmd.clone.sunk | while | flops 246644736 | bytes 12045670 | solution.py:214
  1881.0 13.2 while.143
  1894.3 87.3 %collective-permute-done.4 = bf16[2,1,384,30,128]{4,2,3,1,0:T(8,128)(2,1)} collective-permute-done((bf16[2,1,384,30,128]{4,2,3,1,0:T(8,128)(2,1)}, bf16[2,1,384,30,128]{4,2,3,1,0:T(8,128)(2,1)}, u32[]{:S(2)}, u32[]{:S(2)}) %collective-permute-start.4) | collective-permute-done | bytes 5898272 | tf_op jit(solution)/shard_map/ppermute | solution.py:20
  1991.7 20.3 while.137
  1994.9 6.3 while.146
  2005.1 6.3 while.146
  2017.8 17.5 while.139
  2020.2 6.3 while.147
  2028.8 6.3 while.147
  2050.2 9.3 fusion.191
  2068.8 43.4 %while.133 = (s32[]{:T(128)}, bf16[2,3,128,128]{3,2,1,0:T(8,128)(2,1)}, bf16[2,3,128,128]{3,2,1,0:T(8,128)(2,1)S(1)}, bf16[2,10368,128]{2,1,0:T(8,128)(2,1)}, pr...) while((s32[]{:T(128)}, ...), condition=%wide.region_17.21_spmd.clone, body=%wide.region_10.20_spmd.clone.sunk | while | flops 705822720 | bytes 33300324 | solution.py:214
  2073.6 16.3 while.144
  2095.2 16.3 while.144
  (862 shorter events, 358.9 us)
Async XLA Ops:
  7.2 1675.4 %all-reduce.2.cloned.1.call-start = ((), (), s32[]{:S(2)}) async-start(), calls=%async_computation | async-start | bytes 3145728 | tf_op jit(solution)/shard_map/psum | solution.py:268
  13.9 20.0 copy-start.96
  13.9 21.2 copy-start.87
  17.0 18.0 copy-start.91
  17.0 18.2 copy-start.84
  30.9 1810.3 %copy-start.9 = (bf16[2,2,384,128]{3,2,1,0:T(8,128)(2,1)}, bf16[2,2,384,128]{3,2,1,0:T(8,128)(2,1)S(1)}, u32[]{:S(2)}) copy-start(bf16[2,2,384,128]{3,2,1,0:T(8,128)(2,1)S(1)} %gather_fusion.2) | copy-start | bytes 1179652
  36.8 1647.2 %collective-permute-start.1 = (bf16[2,1,384,8,128]{4,2,0,3,1:T(8,128)(2,1)}, bf16[2,1,384,8,128]{4,2,0,3,1:T(8,128)(2,1)}, u32[]{:S(2)}, u32[]{:S(2)}) collective-permute-start(bf16[2,1,384,8,128]{4,2,0,3,1:T(8,128)(2,1)} %pad_maximum_fusion.2), channel_id=1, source_target_pairs={{1,0},{2,1},{3,2},{4,3},{5,4},{6,5},{7,6},{8,7},{9,8},{10,9},{11,1... | collective-permute-start | bytes 4718600 | tf_op jit(solution)/shard_map/ppermute | solution.py:31
  46.9 1639.4 %collective-permute-start = (bf16[2,1,384,8,128]{4,2,0,3,1:T(8,128)(2,1)}, bf16[2,1,384,8,128]{4,2,0,3,1:T(8,128)(2,1)}, u32[]{:S(2)}, u32[]{:S(2)}) collective-permute-start(bf16[2,1,384,8,128]{4,2,0,3,1:T(8,128)(2,1)} %pad_maximum_fusion.2), channel_id=1, source_target_pairs={{0,1},{1,2},{2,3},{3,4},{4,5},{5,6},{6,7},{7,8},{8,9},{9,10},{10,1... | collective-permute-start | bytes 4718600 | tf_op jit(solution)/shard_map/ppermute | solution.py:31
  50.5 864.7 %copy-start.103 = (bf16[1,1536]{1,0:T(2,128)(2,1)S(1)}, bf16[1,1536]{1,0:T(2,128)(2,1)}, u32[]{:S(2)}) copy-start(bf16[1,1536]{1,0:T(2,128)(2,1)} %param.45) | copy-start | bytes 9220
  915.2 405.3 %copy-start.13 = (f32[1,1,384,1536]{2,3,1,0:T(8,128)S(1)}, f32[1,1,384,1536]{2,3,1,0:T(8,128)}, u32[]{:S(2)}) copy-start(f32[1,1,384,1536]{2,3,1,0:T(8,128)} %copy-done.12) | copy-start | bytes 7077892
  915.2 405.3 %copy-start.80 = (f32[384,12]{0,1:T(8,128)S(1)}, f32[384,12]{0,1:T(8,128)}, u32[]{:S(2)}) copy-start(f32[384,12]{0,1:T(8,128)} %add_sqrt_fusion) | copy-start | bytes 55300
  1427.3 20.5 copy-start.57
  1432.3 125.9 %copy-start.89 = (pred[2]{0:T(512)(128)(4,1)}, pred[2]{0:T(512)(128)(4,1)S(1)}, u32[]{:S(2)}) copy-start(pred[2]{0:T(512)(128)(4,1)S(1)} %get-tuple-element.1122) | copy-start | bytes 10
  1478.9 207.4 %copy-start.21 = (bf16[2,2,384,128]{3,2,1,0:T(8,128)(2,1)}, bf16[2,2,384,128]{3,2,1,0:T(8,128)(2,1)S(1)}, u32[]{:S(2)}) copy-start(bf16[2,2,384,128]{3,2,1,0:T(8,128)(2,1)S(1)} %gather_fusion.6) | copy-start | bytes 1179652
  1692.0 141.7 %collective-permute-start.3 = (bf16[2,1,384,16,128]{4,2,0,3,1:T(8,128)(2,1)}, bf16[2,1,384,16,128]{4,2,0,3,1:T(8,128)(2,1)}, u32[]{:S(2)}, u32[]{:S(2)}) collective-permute-start(bf16[2,1,384,16,128]{4,2,0,3,1:T(8,128)(2,1)} %pad_maximum_fusion.1), channel_id=1, source_target_pairs={{8,0},{9,1},{10,2},{11,3},{12,4},{13,5},{14,6},{15,7},{16,8},{17,9... | collective-permute-start | bytes 9437192 | tf_op jit(solution)/shard_map/ppermute | solution.py:31
  1696.4 138.5 %collective-permute-start.2 = (bf16[2,1,384,16,128]{4,2,0,3,1:T(8,128)(2,1)}, bf16[2,1,384,16,128]{4,2,0,3,1:T(8,128)(2,1)}, u32[]{:S(2)}, u32[]{:S(2)}) collective-permute-start(bf16[2,1,384,16,128]{4,2,0,3,1:T(8,128)(2,1)} %pad_maximum_fusion.1), channel_id=1, source_target_pairs={{0,8},{1,9},{2,10},{3,11},{4,12},{5,13},{6,14},{7,15},{8,16},{9,17... | collective-permute-start | bytes 9437192 | tf_op jit(solution)/shard_map/ppermute | solution.py:31
  1701.3 22.9 %copy-start.31 = (bf16[2,1,384,1,2,128]{5,2,0,4,3,1:T(8,128)(2,1)S(1)}, bf16[2,1,384,1,2,128]{5,2,0,4,3,1:T(8,128)(2,1)}, u32[]{:S(2)}) copy-start(bf16[2,1,384,1,2,128]{5,2,0,4,3,1:T(8,128)(2,1)} %get-tuple-element.1090) | copy-start | bytes 1179652
  1701.3 22.9 %copy-start.33 = (bf16[2,1,384,1,2,128]{5,2,0,4,3,1:T(8,128)(2,1)S(1)}, bf16[2,1,384,1,2,128]{5,2,0,4,3,1:T(8,128)(2,1)}, u32[]{:S(2)}) copy-start(bf16[2,1,384,1,2,128]{5,2,0,4,3,1:T(8,128)(2,1)} %get-tuple-element.1086) | copy-start | bytes 1179652
  1725.5 110.7 %copy-start.54 = (bf16[2,1,384,1,2,128]{5,2,0,4,3,1:T(8,128)(2,1)S(1)}, bf16[2,1,384,1,2,128]{5,2,0,4,3,1:T(8,128)(2,1)}, u32[]{:S(2)}) copy-start(bf16[2,1,384,1,2,128]{5,2,0,4,3,1:T(8,128)(2,1)} %fusion.231) | copy-start | bytes 1179652
  1848.6 136.1 %collective-permute-start.5 = (bf16[2,1,384,30,128]{4,2,3,1,0:T(8,128)(2,1)}, bf16[2,1,384,30,128]{4,2,3,1,0:T(8,128)(2,1)}, u32[]{:S(2)}, u32[]{:S(2)}) collective-permute-start(bf16[2,1,384,30,128]{4,2,3,1,0:T(8,128)(2,1)} %pad_maximum_fusion), channel_id=1, source_target_pairs={{64,0},{128,64},{192,128},{65,1},{129,65},{193,129},{66,2},{130,66... | collective-permute-start | bytes 17694728 | tf_op jit(solution)/shard_map/ppermute | solution.py:23
  1850.8 130.7 %collective-permute-start.4 = (bf16[2,1,384,30,128]{4,2,3,1,0:T(8,128)(2,1)}, bf16[2,1,384,30,128]{4,2,3,1,0:T(8,128)(2,1)}, u32[]{:S(2)}, u32[]{:S(2)}) collective-permute-start(bf16[2,1,384,30,128]{4,2,3,1,0:T(8,128)(2,1)} %pad_maximum_fusion), channel_id=1, source_target_pairs={{0,64},{64,128},{128,192},{1,65},{65,129},{129,193},{2,66},{66,130... | collective-permute-start | bytes 17694728 | tf_op jit(solution)/shard_map/ppermute | solution.py:20
  1858.9 22.0 %copy-start.98 = (pred[1152]{0:T(1024)(128)(4,1)S(1)}, pred[1152]{0:T(1024)(128)(4,1)}, u32[]{:S(2)}) copy-start(pred[1152]{0:T(1024)(128)(4,1)} %broadcast_in_dim.341) | copy-start | bytes 3460
  1858.9 22.1 %copy-start.44 = (bf16[1,384,2,128]{3,1,2,0:T(8,128)(2,1)S(1)}, bf16[1,384,2,128]{3,1,2,0:T(8,128)(2,1)}, u32[]{:S(2)}) copy-start(bf16[1,384,2,128]{3,1,2,0:T(8,128)(2,1)} %bitcast_select_fusion.6) | copy-start | bytes 589828
  1894.3 89.1 %copy-start.61 = (bf16[2,3,128,128]{3,2,1,0:T(8,128)(2,1)}, bf16[2,3,128,128]{3,2,1,0:T(8,128)(2,1)S(1)}, u32[]{:S(2)}) copy-start(bf16[2,3,128,128]{3,2,1,0:T(8,128)(2,1)S(1)} %get-tuple-element.588) | copy-start | bytes 589828
  (111 other events, 438.9 us)
Sparse Core Ops, SparseCore 0:
  1427.5 255.0 all-reduce.1
where the time goes:
time: 2140 us; the launch traced here: 2130 us
  blocking collectives  1430 us (67%)
  waiting for transfers between devices  318 us (15%)
  local copies, waits for them, and re-layouts  166 us (8%)
  other arithmetic  88.6 us (4%)
  matrix products  75.9 us (4%)
  starting transfers between devices  25.6 us (1%)
    all_gather x1, blocking collectives, local(): lax.all_gather(text_parts[0], ('ta', 'sa'), axis=0, tiled=True)  473 us
    all_gather x1, blocking collectives, local(): lax.all_gather(text_parts[2], ('ta', 'sa'), axis=0, tiled=True)  404 us
    all_gather x1, blocking collectives, local(): lax.all_gather(text_parts[1], ('ta', 'sa'), axis=0, tiled=True)  391 us
    psum x1, waiting for transfers between devices, local(): lax.psum((scaled_sums, scaled_totals), ('ta', 'sa'))  123 us
    ppermute x4, waiting for transfers between devices, shifted(): lax.ppermute(value, axis, [(source, source + steps) for source in range(i...  108 us
    pmax x1, blocking collectives, local(): peak_value = lax.pmax(joint_peak, ('ta', 'sa'))  93.1 us
    ppermute x1, waiting for transfers between devices, with_halo(): lax.ppermute(lax.slice_in_dim(block, block.shape[dim] - width, None, axis...  87.3 us
    psum x1, blocking collectives, local(): lax.psum((scaled_sums, scaled_totals), ('ta', 'sa'))  73.6 us
  transfers between devices with their start and end apart: 7, of which 3 were waited for; matrix products, arithmetic and copies ran while one was open for 7% of the time, Pallas kernels for 0%

commit v1 on v0

v1 whole, which is shorter than its diff:
```python
import functools
import math

import jax
import jax.numpy as jnp
from jax import lax
from jax.experimental import pallas as pl
from jax.experimental.pallas import tpu as pltpu
from jax.sharding import PartitionSpec as P

MESH = pl.DeviceIdType.MESH
EPS = 1e-6
F32, BF16 = jnp.float32, jnp.bfloat16
HEADS, D, TOK, TEXT = 12, 128, 384, 256
SW = 8
BIG = 1e30
TROWS = 48
VMEM_LIMIT = 61 * 2**20
RANK_OF_CODE = (0, 0, 5, 1, 0, 3, 4, 2)


def pre_kernel(order, vq, vk, vv, tq, tk, tv, qg, kg, q_out, kv_out, t_out, rows):
    i = pl.program_id(0)

    def norm(value, gain):
        u = value.astype(F32)
        spread = jnp.sqrt(jnp.mean(u * u, axis=-1, keepdims=True) + EPS)
        return u / spread * gain

    @pl.when(i == 0)
    def _():
        rows[...] = jnp.zeros_like(rows)

    q_out[0] = norm(vq[0, 0], qg[...]).astype(BF16)
    kv_out[0, 0] = norm(vk[0, 0], kg[...]).astype(BF16)
    kv_out[0, 1] = vv[0, 0]
    rows[pl.ds(i, 1), :] = norm(tq[...], qg[...])
    rows[pl.ds(HEADS + i, 1), :] = norm(tk[...], kg[...])
    rows[pl.ds(2 * HEADS + i, 1), :] = tv[...].astype(F32)

    @pl.when(i == HEADS - 1)
    def _():
        t_out[...] = rows[...].astype(BF16)


def post_kernel(order, vo, to, v_out, t_out):
    i = pl.program_id(0)
    v_out[0, 0] = vo[0]
    t_out[...] = to[pl.ds((i // 6) * 8 + i % 6, 1), :].astype(BF16)


def merge(o1, l1, o2, l2):
    top = jnp.maximum(l1, l2)
    w1 = jnp.exp2(l1 - top)
    w2 = jnp.exp2(l2 - top)
    total = w1 + w2
    return (o1 * w1 + o2 * w2) / total, top + jnp.log2(total)


def dot_t(a, b):
    return lax.dot_general(a, b, (((1,), (1,)), ((), ())), preferred_element_type=F32)


def attend(q, pieces):
    cc = math.log2(math.e) / math.sqrt(D)
    scores, peak = [], None
    for k, v, penalty, bias in pieces:
        s = dot_t(q, k)
        if bias is not None:
            s = s + bias
        scores.append(s)
        row = jnp.max(s, axis=-1, keepdims=True)
        if penalty is not None:
            row = row - penalty
        peak = row if peak is None else jnp.maximum(peak, row)
    peak = peak * cc
    total = None
    for s, (k, v, penalty, bias) in zip(scores, pieces):
        shift = peak if penalty is None else peak + penalty
        w = jnp.exp2(s * cc - shift).astype(BF16)
        ones = jnp.ones(v.shape, BF16)
        part = jnp.dot(w, jnp.concatenate([v, ones], axis=1), preferred_element_type=F32)
        total = part if total is None else total + part
    o, l = total[:, :D], total[:, D:]
    return o / l, peak + jnp.log2(l)


class Copy:
    def __init__(self, sems, number, src, dst, device, sends=None, receives=None):
        self.args = (src, dst, sems[0].at[number], sems[1].at[number])
        self.device, self.sends, self.receives = device, sends, receives

    def act(self, name, condition):
        def go():
            getattr(pltpu.make_async_remote_copy(
                *self.args, device_id=self.device, device_id_type=MESH), name)()
        if condition is None:
            go()
        else:
            pl.when(condition)(go)

    def start(self):
        self.act("start", self.sends)

    def wait_send(self):
        self.act("wait_send", self.sends)

    def wait_recv(self):
        self.act("wait_recv", self.receives)


def main_kernel(q_in, kv_in, t_in, tlen, v_out, t_out,
                q_all, kvg, o_own, l_own, o_send, l_send, o_got, l_got,
                tg, tf, tx, tp, ta, tb, td, te, rc, rx, ry, rz, re,
                own_sem, ssem, rsem, ret_s, ret_r):
    t = lax.axis_index("ta")
    s = lax.axis_index("sa")
    a, b, c = s // SW, s % SW, s % 2
    x, y, zh = s // 16, (s // 4) % 4, (s // 2) % 2
    z = zh * 4 + t
    has_out = jnp.where(c == 0, b > 0, b < SW - 1)
    mate = (t, s + 1 - 2 * c)
    outd = (t, s - 1 + 2 * c)
    t_up, t_dn, r_up, r_dn = t < 3, t > 0, a < 7, a > 0
    d_tup, d_tdn, d_rup, d_rdn = (t + 1, s), (t - 1, s), (t, s + SW), (t, s - SW)
    peers = {"x": [], "y": [], "z": []}
    for i in range(1, 4):
        x2, y2 = (x + i) % 4, (y + i) % 4
        peers["x"].append((x2, (t, s + 16 * (x2 - x))))
        peers["y"].append((y2, (t, s + 4 * (y2 - y))))
    for i in range(1, 8):
        z2 = (z + i) % 8
        peers["z"].append((z2, (z2 % 4, s + 2 * (z2 // 4 - zh))))

    bar = pltpu.get_barrier_semaphore()

    def greet(device, exists=None):
        def go():
            pl.semaphore_signal(bar, inc=1, device_id=device, device_id_type=MESH)
        if exists is None:
            go()
        else:
            pl.when(exists)(go)

    greet(mate)
    greet(outd, has_out)
    greet(d_tup, t_up)
    greet(d_tdn, t_dn)
    greet(d_rup, r_up)
    greet(d_rdn, r_dn)
    for axis in "xyz":
        for _, device in peers[axis]:
            greet(device)

    gi = c * 128 + (x * 4 + y) * 8 + z
    locals_ = [
        pltpu.make_async_copy(kv_in, kvg.at[pl.ds(0, HEADS), 0], own_sem.at[0]),
        pltpu.make_async_copy(q_in, q_all.at[0], own_sem.at[1]),
        pltpu.make_async_copy(t_in, tg.at[gi], own_sem.at[2]),
    ]
    for item in locals_:
        item.start()

    @pl.when(jnp.logical_not(has_out))
    def _():
        for h in range(8):
            kvg[h, 1] = jnp.zeros((2, TOK, D), BF16)
        for g in range(4):
            kvg[12 + g, 1] = jnp.zeros((2, TOK, D), BF16)

    @pl.when(jnp.logical_not(r_dn))
    def _():
        for h in range(8, 12):
            kvg[h, 1] = jnp.zeros((2, TOK, D), BF16)

    @pl.when(jnp.logical_not(r_up))
    def _():
        for h in range(8, 12):
            kvg[h, 2] = jnp.zeros((2, TOK, D), BF16)

    count = 14 + has_out.astype(jnp.int32) + t_up.astype(jnp.int32) + t_dn.astype(jnp.int32)
    count = count + r_up.astype(jnp.int32) + r_dn.astype(jnp.int32)
    pl.semaphore_wait(bar, count)

    sems = (ssem, rsem)
    number = [0]

    def copy(src, dst, device, sends=None, receives=None):
        number[0] += 1
        return Copy(sems, number[0] - 1, src, dst, device, sends, receives)

    def both(src, dst_low, dst_high, axis):
        if axis == "t":
            return [copy(src, dst_low, d_tup, t_up, t_dn), copy(src, dst_high, d_tdn, t_dn, t_up)]
        return [copy(src, dst_low, d_rup, r_up, r_dn), copy(src, dst_high, d_rdn, r_dn, r_up)]

    def heads(first, n):
        return pl.ds(first, n)

    out_c0 = copy(kv_in.at[heads(4, 2)], kvg.at[heads(4, 2), 1], outd, has_out, has_out)
    out_c12 = [copy(kv_in.at[heads(2, 2)], kvg.at[heads(2, 2), 1], outd, has_out, has_out),
               copy(kv_in.at[heads(6, 2)], kvg.at[heads(6, 2), 1], outd, has_out, has_out)]
    out_c4 = copy(kv_in.at[heads(0, 2)], kvg.at[heads(0, 2), 1], outd, has_out, has_out)
    mate_kv = copy(kv_in.at[heads(0, 8)], kvg.at[heads(0, 8), 2], mate)
    rows_kv = both(kv_in.at[heads(8, 4)], kvg.at[heads(8, 4), 1], kvg.at[heads(8, 4), 2], "r")
    relay_own = both(kv_in.at[4], kvg.at[12, 0], kvg.at[13, 0], "t") + both(kv_in.at[5], kvg.at[14, 0], kvg.at[15, 0], "r")

    def both_out(src, dst_low, dst_high, axis):
        up, dn, dev_up, dev_dn = (t_up, t_dn, d_tup, d_tdn) if axis == "t" else (r_up, r_dn, d_rup, d_rdn)
        return [copy(src, dst_low, dev_up, up & has_out, dn & has_out),
                copy(src, dst_high, dev_dn, dn & has_out, up & has_out)]

    relay_out = both_out(kvg.at[4, 1], kvg.at[12, 1], kvg.at[13, 1], "t") + both_out(kvg.at[5, 1], kvg.at[14, 1], kvg.at[15, 1], "r")
    exists = [t_dn, t_up, r_dn, r_up]
    relay_mate = [copy(kvg.at[12 + g, 0], kvg.at[12 + g, 2], mate, exists[g], exists[g]) for g in range(4)]
    q_row = both(q_in.at[heads(2, 3)], q_all.at[1, heads(2, 3)], q_all.at[2, heads(2, 3)], "r")
    q_time = both(q_in.at[heads(5, 5)], q_all.at[1, heads(5, 5)], q_all.at[2, heads(5, 5)], "t")
    g_z = [copy(tg.at[gi], tg.at[gi], device) for _, device in peers["z"]]
    base_y, base_x = c * 128 + (x * 4 + y) * 8, c * 128 + x * 32
    g_y = [copy(tg.at[pl.ds(base_y, 8)], tg.at[pl.ds(base_y, 8)], device) for _, device in peers["y"]]
    g_x = [copy(tg.at[pl.ds(base_x, 32)], tg.at[pl.ds(base_x, 32)], device) for _, device in peers["x"]]
    g_c = copy(tg.at[pl.ds(c * 128, 128)], tg.at[pl.ds(c * 128, 128)], mate)
    s_c = copy(tp.at[pl.ds(6 * (1 - c), 6)], rc, mate)
    s_x = [copy(ta.at[:, :, :, x2], rx.at[i], device) for i, (x2, device) in enumerate(peers["x"])]
    s_y = [copy(tb.at[:, :, :, pl.ds(8 * y2, 8)], ry.at[i], device) for i, (y2, device) in enumerate(peers["y"])]
    s_z = [copy(td.at[z2], rz.at[i], device) for i, (z2, device) in enumerate(peers["z"])]
    s_e = copy(te.at[pl.ds(8 * (1 - c), 8)], re, mate)

    def start(items):
        for item in items:
            item.start()

    def got(items):
        for item in items:
            item.wait_recv()

    def sent(items):
        for item in items:
            item.wait_send()

    for item in locals_:
        item.wait()
    start(g_z)
    start([out_c0])
    start(rows_kv + q_time + q_row + relay_own + [mate_kv] + out_c12 + [out_c4])

    pen_out = jnp.where(has_out, 0.0, BIG).astype(F32)
    pen_rdn = jnp.where(r_dn, 0.0, BIG).astype(F32)
    pen_rup = jnp.where(r_up, 0.0, BIG).astype(F32)
    bias_idx = lax.broadcasted_iota(jnp.int32, (1, TEXT), 1)
    i_c, i_x, i_y, i_z = bias_idx // 128, (bias_idx // 32) % 4, (bias_idx // 8) % 4, bias_idx % 8
    original = (i_z % 4) * 64 + i_x * 16 + i_y * 4 + (i_z // 4) * 2 + i_c
    text_bias = jnp.where(original < tlen[0], 0.0, -BIG).astype(F32)

    def text_arrived():
        def widen(i, _):
            tf[pl.ds(pl.multiple_of(i * 8 * TROWS, 8 * TROWS), 8 * TROWS)] = (
                tg[pl.ds(i * 8, 8)].astype(F32).reshape(8 * TROWS, D))
            return 0
        lax.fori_loop(0, TEXT // 8, widen, 0)

        def pick(j, _):
            tx[j] = tf[pl.ds(j, TEXT, stride=TROWS), :].astype(BF16)
            return 0
        lax.fori_loop(0, 3 * HEADS, pick, 0)

        def partial(h, _):
            o, l = attend(tx[h], [(kvg[h, 0, 0], kvg[h, 0, 1], None, None)])
            tp[h, 0] = o.reshape(2, 4, 32, D)
            tp[h, 1] = jnp.broadcast_to(l, (TEXT, D)).reshape(2, 4, 32, D)
            return 0
        lax.fori_loop(0, HEADS, partial, 0)

        @pl.when((t == 0) & (s == 0))
        def _():
            def self_part(h, _):
                o, l = attend(tx[h], [(tx[HEADS + h], tx[2 * HEADS + h], None, text_bias)])
                o, l = merge(tp[h, 0].reshape(TEXT, D), tp[h, 1].reshape(TEXT, D), o, l)
                tp[h, 0] = o.reshape(2, 4, 32, D)
                tp[h, 1] = l.reshape(2, 4, 32, D)
                return 0
            lax.fori_loop(0, HEADS, self_part, 0)

    def reduce_c():
        def one(h, _):
            o, l = merge(tp[6 * c + h, 0], tp[6 * c + h, 1], rc[h, 0], rc[h, 1])
            ta[h, 0] = o
            ta[h, 1] = l
            return 0
        lax.fori_loop(0, 6, one, 0)

    def reduce_x():
        def one(h, _):
            o, l = ta[h, 0, :, x], ta[h, 1, :, x]
            for i in range(3):
                o, l = merge(o, l, rx[i, h, 0], rx[i, h, 1])
            tb[h, 0] = o
            tb[h, 1] = l
            return 0
        lax.fori_loop(0, 6, one, 0)

    def reduce_y():
        for h in range(6):
            for cc in range(2):
                rows = pl.ds(pl.multiple_of(8 * y, 8), 8)
                o, l = tb[h, 0, cc, rows], tb[h, 1, cc, rows]
                for i in range(3):
                    o, l = merge(o, l, ry[i, h, 0, cc], ry[i, h, 1, cc])
                for k, value in enumerate((o, l)):
                    for zz in range(8):
                        td[zz, pl.ds(k * 16 + cc * 8 + h, 1), :] = value[zz:zz + 1]

    def reduce_z():
        o, l = td[z, pl.ds(0, 16)], td[z, pl.ds(16, 16)]
        for i in range(7):
            o, l = merge(o, l, rz[i, pl.ds(0, 16)], rz[i, pl.ds(16, 16)])
        te[...] = o

    def spread_out(l):
        return jnp.transpose(jnp.broadcast_to(l, (D, TOK)))

    def return_copies(h, d):
        row = h < 5
        dev_t = jnp.where(row, t, t - 1 + 2 * d)
        dev_s = jnp.where(row, s + (2 * d - 1) * SW, s)
        device = (dev_t, dev_s)
        return [
            pltpu.make_async_remote_copy(src_ref=o_send.at[d, h - 2], dst_ref=o_got.at[1 - d, h - 2],
                                         send_sem=ret_s.at[0, d, h - 2], recv_sem=ret_r.at[0, 1 - d, h - 2],
                                         device_id=device, device_id_type=MESH),
            pltpu.make_async_remote_copy(src_ref=l_send.at[d, h - 2], dst_ref=l_got.at[1 - d, h - 2],
                                         send_sem=ret_s.at[1, d, h - 2], recv_sem=ret_r.at[1, 1 - d, h - 2],
                                         device_id=device, device_id_type=MESH),
        ]

    def there(h, d):
        row = h < 5
        low = jnp.where(row, a, t) > 0
        high = jnp.where(row, a - 4, t) < 3
        return (h >= 2) & (h < 10) & jnp.where(d == 0, low, high)

    events = {
        0: lambda: (got(g_z), start(g_y), got(rows_kv), got(q_time)),
        1: lambda: (got(g_y), sent(g_z), start(g_x)),
        2: lambda: (got([out_c0]), start(relay_out)),
        3: lambda: (got(relay_own), start(relay_mate)),
        4: lambda: (got([mate_kv]), got(q_row), got(out_c12)),
        5: lambda: (got(g_x), sent(g_y), start([g_c])),
        6: lambda: (got([g_c]), text_arrived(), start([s_c])),
        7: lambda: (got([s_c]), reduce_c(), start(s_x)),
        8: lambda: (got(relay_out), got(relay_mate)),
        9: lambda: (got(s_x), reduce_x(), start(s_y)),
        10: lambda: (got([out_c4]),),
        11: lambda: (got(s_y), reduce_y(), start(s_z)),
    }

    def step(n, _):
        pair = n // 2
        first = jnp.where(pair == 0, 8, jnp.where(pair == 1, 10, jnp.where(pair == 2, 2, jnp.where(
            pair == 3, 6, jnp.where(pair == 4, 4, 0)))))
        h = first + n % 2
        for at, event in events.items():
            pl.when(n == at)(functools.partial(lambda event: event() and None, event))
        pen_a = jnp.where(h < 8, pen_out, pen_rdn)
        pen_b = jnp.where(h < 8, 0.0, pen_rup)
        relayed = pair == 4

        def one_query(qd, _):
            @pl.when((qd == 0) | there(h, qd - 1))
            def _():
                q = q_all[qd, h]

                def one_group(g, _):
                    group = jnp.where(g == 0, h, 12 + (h - 4) * 2 + g - 1)
                    present = jnp.where(h == 4, jnp.where(g == 1, t, 3 - t), jnp.where(g == 1, a, 7 - a)) > 0

                    @pl.when((g == 0) | present)
                    def _():
                        o, l = attend(q, [
                            (kvg[group, 0, 0], kvg[group, 0, 1], None, None),
                            (kvg[group, 1, 0], kvg[group, 1, 1], pen_a, None),
                            (kvg[group, 2, 0], kvg[group, 2, 1], pen_b, None),
                        ])

                        @pl.when(g == 0)
                        def _():
                            o_own[qd, h] = o
                            l_own[qd, h] = l

                        @pl.when(g > 0)
                        def _():
                            o2, l2 = merge(o_own[qd, h], l_own[qd, h], o, l)
                            o_own[qd, h] = o2
                            l_own[qd, h] = l2
                    return 0

                lax.fori_loop(0, jnp.where(relayed, 3, 1), one_group, 0)

                @pl.when(qd > 0)
                def _():
                    d = qd - 1
                    o_send[d, h - 2] = o_own[qd, h].astype(BF16)
                    l_send[d, h - 2] = jnp.transpose(l_own[qd, h])[:8]
                    for item in return_copies(h, d):
                        item.start()
            return 0

        lax.fori_loop(0, jnp.where((h >= 2) & (h < 10), 3, 1), one_query, 0)
        return 0

    lax.fori_loop(0, 12, step, 0)

    got(s_z)
    reduce_z()
    start([s_e])

    def finish(n, _):
        pair = n // 2
        first = jnp.where(pair == 0, 0, jnp.where(pair == 1, 10, jnp.where(pair == 2, 8, jnp.where(
            pair == 3, 2, jnp.where(pair == 4, 6, 4)))))
        h = first + n % 2
        o, l = attend(q_all[0, h], [(tx[HEADS + h], tx[2 * HEADS + h], None, text_bias)])
        o, l = merge(o_own[0, h], l_own[0, h], o, l)
        o_own[0, h] = o
        l_own[0, h] = l
        for d in range(2):
            @pl.when(there(h, d))
            def _():
                for item in return_copies(h, 1 - d):
                    item.wait_recv()
                o2, l2 = merge(o_own[0, h], l_own[0, h], o_got[d, h - 2].astype(F32),
                               spread_out(l_got[d, h - 2][:1]))
                o_own[0, h] = o2
                l_own[0, h] = l2
                for item in return_copies(h, d):
                    item.wait_send()
        v_out[h] = o_own[0, h].astype(BF16)
        return 0

    lax.fori_loop(0, 12, finish, 0)

    got([s_e])
    t_out[pl.ds(pl.multiple_of(8 * c, 8), 8), :] = te[pl.ds(pl.multiple_of(8 * c, 8), 8), :]
    t_out[pl.ds(pl.multiple_of(8 - 8 * c, 8), 8), :] = re[...]
    sent([out_c0, out_c4, mate_kv, g_c, s_c, s_e] + out_c12 + rows_kv + relay_own + relay_out + relay_mate)
    sent(q_row + q_time + g_x + s_x + s_y + s_z)


N_COPIES = 64


def main_call(q, kv, text, text_len):
    shapes = [
        pltpu.VMEM((3, HEADS, TOK, D), BF16),
        pltpu.VMEM((16, 3, 2, TOK, D), BF16),
        pltpu.VMEM((3, HEADS, TOK, D), F32),
        pltpu.VMEM((3, HEADS, TOK, D), F32),
        pltpu.VMEM((2, 8, TOK, D), BF16),
        pltpu.VMEM((2, 8, 8, TOK), F32),
        pltpu.VMEM((2, 8, TOK, D), BF16),
        pltpu.VMEM((2, 8, 8, TOK), F32),
        pltpu.VMEM((TEXT, TROWS, D), BF16),
        pltpu.VMEM((TEXT * TROWS, D), F32),
        pltpu.VMEM((3 * HEADS, TEXT, D), BF16),
        pltpu.VMEM((HEADS, 2, 2, 4, 32, D), F32),
        pltpu.VMEM((6, 2, 2, 4, 32, D), F32),
        pltpu.VMEM((6, 2, 2, 32, D), F32),
        pltpu.VMEM((8, 32, D), F32),
        pltpu.VMEM((16, D), F32),
        pltpu.VMEM((6, 2, 2, 4, 32, D), F32),
        pltpu.VMEM((3, 6, 2, 2, 32, D), F32),
        pltpu.VMEM((3, 6, 2, 2, 8, D), F32),
        pltpu.VMEM((7, 32, D), F32),
        pltpu.VMEM((8, D), F32),
        pltpu.SemaphoreType.DMA((3,)),
        pltpu.SemaphoreType.DMA((N_COPIES,)),
        pltpu.SemaphoreType.DMA((N_COPIES,)),
        pltpu.SemaphoreType.DMA((2, 2, 8)),
        pltpu.SemaphoreType.DMA((2, 2, 8)),
    ]
    anywhere = pl.BlockSpec(memory_space=pl.ANY)
    return pl.pallas_call(
        main_kernel,
        out_shape=(jax.ShapeDtypeStruct((HEADS, TOK, D), BF16), jax.ShapeDtypeStruct((16, D), F32)),
        in_specs=[anywhere, anywhere, anywhere, pl.BlockSpec(memory_space=pltpu.SMEM)],
        out_specs=(pl.BlockSpec(memory_space=pltpu.VMEM), pl.BlockSpec(memory_space=pltpu.VMEM)),
        scratch_shapes=shapes,
        compiler_params=pltpu.CompilerParams(
            collective_id=0, has_side_effects=True, vmem_limit_bytes=VMEM_LIMIT),
        name="tiles",
    )(q, kv, text, text_len)


def local(video_q, video_k, video_v, text_q, text_k, text_v, q_gain, k_gain, text_len, window):
    wide = (window == 3).astype(jnp.int32)
    code = wide[:, 0] * 4 + wide[:, 1] * 2 + wide[:, 2]
    rank = jnp.zeros_like(code)
    for value, place in enumerate(RANK_OF_CODE):
        rank = jnp.where(code == value, place, rank)
    key = rank * HEADS + jnp.arange(HEADS, dtype=jnp.int32)
    position = jnp.sum((key[None, :] < key[:, None]).astype(jnp.int32), axis=1)
    places = jnp.arange(HEADS, dtype=jnp.int32)
    order = jnp.sum(jnp.where(position[None, :] == places[:, None], places[None, :], 0), axis=1)

    tile = pl.BlockSpec((1, 1, TOK, D), lambda i, order: (0, 0, 0, order[i]))
    row = pl.BlockSpec((1, D), lambda i, order: (0, order[i]))
    gain = pl.BlockSpec((1, D), lambda i, order: (0, 0))
    q, kv, text = pl.pallas_call(
        pre_kernel,
        grid_spec=pltpu.PrefetchScalarGridSpec(
            num_scalar_prefetch=1, grid=(HEADS,),
            in_specs=[tile, tile, tile, row, row, row, gain, gain],
            out_specs=[
                pl.BlockSpec((1, TOK, D), lambda i, order: (i, 0, 0)),
                pl.BlockSpec((1, 2, TOK, D), lambda i, order: (i, 0, 0, 0)),
                pl.BlockSpec((TROWS, D), lambda i, order: (0, 0)),
            ],
            scratch_shapes=[pltpu.VMEM((TROWS, D), F32)],
        ),
        out_shape=(jax.ShapeDtypeStruct((HEADS, TOK, D), BF16), jax.ShapeDtypeStruct((HEADS, 2, TOK, D), BF16),
                   jax.ShapeDtypeStruct((TROWS, D), BF16)),
        name="prepare",
    )(order, video_q, video_k, video_v, text_q, text_k, text_v, q_gain[None], k_gain[None])

    video, text_rows = main_call(q, kv, text, text_len)

    return tuple(pl.pallas_call(
        post_kernel,
        grid_spec=pltpu.PrefetchScalarGridSpec(
            num_scalar_prefetch=1, grid=(HEADS,),
            in_specs=[pl.BlockSpec((1, TOK, D), lambda i, order: (i, 0, 0)),
                      pl.BlockSpec((16, D), lambda i, order: (0, 0))],
            out_specs=[tile, row],
        ),
        out_shape=(jax.ShapeDtypeStruct(video_q.shape, BF16), jax.ShapeDtypeStruct(text_q.shape, BF16)),
        name="place",
    )(order, video, text_rows))


def solution(mesh):
    tiles, rows = P("ta", "sa", None, None), P(("ta", "sa"), None)
    return jax.shard_map(
        local, mesh=mesh,
        in_specs=(tiles, tiles, tiles, rows, rows, rows, P(), P(), P(), P()),
        out_specs=(tiles, rows),
        check_vma=False,
    )
```

time: 2140 us -> 195 us (0.09)
  blocking collectives: 1430 us -> 0 us
  waiting for transfers between devices: 318 us -> 0 us
  Pallas kernels: 0 us -> 192 us
  local copies, waits for them, and re-layouts: 166 us -> 0 us
  other arithmetic: 88.6 us -> 1.49 us
  matrix products: 75.9 us -> 0 us
  starting transfers between devices: 25.6 us -> 0 us
    all_gather x3 -> x0, blocking collectives: 1270 us -> none  [the longest x1 473 us: local(): lax.all_gather(text_parts[0], ('ta', 'sa'), axis=0, tiled=True)]
    ppermute x6 -> x0, waiting for transfers between devices: 195 us -> none  [the longest x4 108 us: shifted(): lax.ppermute(value, axis, [(source, source + steps) for source in range(i...]
    pallas_call x0 -> x3, Pallas kernels: none -> 192 us  [the longest x1 173 us: main_call(): pl.pallas_call(main_kernel, out_shape=(jax.ShapeDtypeStruct((HEADS, TOK,...]
    psum x1 -> x0, waiting for transfers between devices: 123 us -> none  [local(): lax.psum((scaled_sums, scaled_totals), ('ta', 'sa'))]
    pmax x1 -> x0, blocking collectives: 93.1 us -> none  [local(): peak_value = lax.pmax(joint_peak, ('ta', 'sa'))]
    dot_general x148 -> x0, matrix products: 75.9 us -> none  [the longest x36 29.2 us: attend_block(): jnp.einsum('qd,kd->qk', block_queries, item_keys, preferred_element_type=...]
    psum x1 -> x0, blocking collectives: 73.6 us -> none  [local(): lax.psum((scaled_sums, scaled_totals), ('ta', 'sa'))]
    slice x24 -> x0, local copies, waits for them, and re-layouts: 40.9 us -> none  [the longest x12 20.6 us: local(): key_rows[1]]
  transfers between devices with their start and end apart: 7 -> 0, of which waited for: 3 -> 0; matrix products, arithmetic and copies ran while one was open for 7% -> 0% of each run, Pallas kernels for 0% -> 0%
where the time goes in v1:
time: 195 us; the launch traced here: 194 us
  Pallas kernels  192 us (98%)
    pallas_call x1, Pallas kernels, main_call(): pl.pallas_call(main_kernel, out_shape=(jax.ShapeDtypeStruct((HEADS, TOK,...  173 us
    pallas_call x1, Pallas kernels, local(): pl.pallas_call(pre_kernel, grid_spec=pltpu.PrefetchScalarGridSpec(num_sca...  10.4 us
    pallas_call x1, Pallas kernels, local(): pl.pallas_call(post_kernel, grid_spec=pltpu.PrefetchScalarGridSpec(num_sc...  7.89 us

profile of v1, /device:TPU:36, one launch (start us, length us, event | category | flops | bytes accessed | tf_op | source)
XLA Modules:
  0.0 194.4 jit_solution(7969325457989142302)
XLA Ops:
  1.3 0.7 compare_convert_fusion
  2.0 0.2 convert_reduce_fusion
  2.2 0.6 select_reduce_fusion.order
  2.8 10.4 %prepare.1 = (bf16[12,384,128]{2,1,0:T(8,128)(2,1)}, bf16[12,2,384,128]{3,2,1,0:T(8,128)(2,1)}, bf16[48,128]{1,0:T(8,128)(2,1)}) custom-call(s32[12]{0:T(128)} %select_reduce_fusion.order, bf16[1,1,384,1536]{3,2,1,0:T(8,128)(2,1)} %vq.1, bf16[1,1,384,1536]{3,2,1,0:T(8,128)(2,1)} %vk.1, bf16[1,1,384,1536]{3,2,1,0:T(8,128)(2,1)} %vv.1, bf16[1,1536]{1,0:T(2,128)(2,1)} %tq.1, ...), custom_call_target="tpu_custom_call" | custom-call | tf_op jit(solution)/shard_map/prepare/pallas_call | solution.py:508
  13.1 173.3 %tiles.1 = (bf16[12,384,128]{2,1,0:T(8,128)(2,1)}, f32[16,128]{1,0:T(8,128)}) custom-call(bf16[12,384,128]{2,1,0:T(8,128)(2,1)} %get-tuple-element.7.q_in, bf16[12,2,384,128]{3,2,1,0:T(8,128)(2,1)} %get-tuple-element.8.kv_in, bf16[48,128]{1,0:T(8,128)(2,1)} %get-tuple-element.9.t_in, s32[1]{0:T(128)S(6)} %copy.12.tlen), custom_call_target="tpu_custom_call" | custom-call | tf_op jit(solution)/shard_map/tiles/pallas_call | solution.py:482
  186.5 7.9 %place.1 = (bf16[1,1,384,1536]{3,2,1,0:T(8,128)(2,1)}, bf16[1,1536]{1,0:T(2,128)(2,1)}) custom-call(s32[12]{0:T(128)} %select_reduce_fusion.order, bf16[12,384,128]{2,1,0:T(8,128)(2,1)} %get-tuple-element.10.vo, f32[16,128]{1,0:T(8,128)} %get-tuple-element.11.to), custom_call_target="tpu_custom_call" | custom-call | tf_op jit(solution)/shard_map/place/pallas_call | solution.py:527
  (2 shorter events, 0.0 us)

commit v2 on v1

v2 whole, which is shorter than its diff:
```python
import functools
import math

import jax
import jax.numpy as jnp
from jax import lax
from jax.experimental import pallas as pl
from jax.experimental.pallas import tpu as pltpu
from jax.sharding import PartitionSpec as P

MESH = pl.DeviceIdType.MESH
EPS = 1e-6
F32, BF16 = jnp.float32, jnp.bfloat16
HEADS, D, TOK, TEXT = 12, 128, 384, 256
SW = 8
BIG = 1e30
TROWS = 48
VMEM_LIMIT = 61 * 2**20
RANK_OF_CODE = (0, 0, 5, 1, 0, 3, 4, 2)


def merge(o1, l1, o2, l2):
    top = jnp.maximum(l1, l2)
    w1 = jnp.exp2(l1 - top)
    w2 = jnp.exp2(l2 - top)
    total = w1 + w2
    return (o1 * w1 + o2 * w2) / total, top + jnp.log2(total)


def dot_t(a, b):
    return lax.dot_general(a, b, (((1,), (1,)), ((), ())), preferred_element_type=F32)


def attend(q, pieces):
    cc = math.log2(math.e) / math.sqrt(D)
    scores, peak = [], None
    for k, v, penalty, bias in pieces:
        s = dot_t(q, k)
        if bias is not None:
            s = s + bias
        scores.append(s)
        row = jnp.max(s, axis=-1, keepdims=True)
        if penalty is not None:
            row = row - penalty
        peak = row if peak is None else jnp.maximum(peak, row)
    peak = peak * cc
    total = None
    for s, (k, v, penalty, bias) in zip(scores, pieces):
        shift = peak if penalty is None else peak + penalty
        w = jnp.exp2(s * cc - shift).astype(BF16)
        ones = jnp.ones(v.shape, BF16)
        part = jnp.dot(w, jnp.concatenate([v, ones], axis=1), preferred_element_type=F32)
        total = part if total is None else total + part
    o, l = total[:, :D], total[:, D:]
    return o / l, peak + jnp.log2(l)


class Copy:
    def __init__(self, sems, number, src, dst, device, sends=None, receives=None):
        self.args = (src, dst, sems[0].at[number], sems[1].at[number])
        self.device, self.sends, self.receives = device, sends, receives

    def act(self, name, condition):
        def go():
            getattr(pltpu.make_async_remote_copy(
                *self.args, device_id=self.device, device_id_type=MESH), name)()
        if condition is None:
            go()
        else:
            pl.when(condition)(go)

    def start(self):
        self.act("start", self.sends)

    def wait_send(self):
        self.act("wait_send", self.sends)

    def wait_recv(self):
        self.act("wait_recv", self.receives)


def main_kernel(order, place, tlen, vq, vk, vv, tq, tk, tv, qg, kg, v_out, t_out,
                q_all, kvg, rbuf, o_own, l_own, o_send, l_send, o_got, l_got, final,
                raw, raw_t, rows, tg, tf, tx, tpo, tpl, tao, tal, tb, td, te, rco, rcl, rxo, rxl, ry, rz, tr, ends,
                ssem, rsem, ret_s, ret_r):
    t = lax.axis_index("ta")
    s = lax.axis_index("sa")
    a, b, c = s // SW, s % SW, s % 2
    x, y, zh = s // 16, (s // 4) % 4, (s // 2) % 2
    z = zh * 4 + t
    even = a % 2 == 0
    has_out = jnp.where(c == 0, b > 0, b < SW - 1)
    middle, edge = (b == 3) | (b == 4), (b == 0) | (b == SW - 1)
    has_far = jnp.where(even, a >= 2, a <= 5)
    far_send = jnp.where(even, a <= 4, a >= 3)
    t_up, t_dn, r_up, r_dn = t < 3, t > 0, a < 7, a > 0
    mate = (t, s + 1 - 2 * c)
    outd = (t, s - 1 + 2 * c)
    d_tup, d_tdn, d_rup, d_rdn = (t + 1, s), (t - 1, s), (t, s + SW), (t, s - SW)
    pair = (t, jnp.where(even, s + SW, s - SW))
    fard = (t, jnp.where(even, s + 2 * SW, s - 2 * SW))
    via = (t, jnp.where(b == 3, s + 4, s - 4))
    hop = (t, jnp.where(b % 4 == 0, s + 3, s - 3))
    peers = {"x": [], "y": [], "z": []}
    for i in range(1, 4):
        x2, y2 = (x + i) % 4, (y + i) % 4
        peers["x"].append((x2, (t, s + 16 * (x2 - x))))
        peers["y"].append((y2, (t, s + 4 * (y2 - y))))
    for i in range(1, 8):
        z2 = (z + i) % 8
        peers["z"].append((z2, (z2 % 4, s + 2 * (z2 // 4 - zh))))

    bar = pltpu.get_barrier_semaphore()

    def greet(device, exists=None):
        def go():
            pl.semaphore_signal(bar, inc=1, device_id=device, device_id_type=MESH)
        if exists is None:
            go()
        else:
            pl.when(exists)(go)

    greet(mate)
    greet(outd, has_out)
    greet(hop, middle | edge)
    greet(d_tup, t_up)
    greet(d_tdn, t_dn)
    greet(d_rup, r_up)
    greet(d_rdn, r_dn)
    for axis in "xyz":
        for _, device in peers[axis]:
            greet(device)

    sems = (ssem, rsem)
    number = [0]

    def copy(src, dst, device, sends=None, receives=None):
        number[0] += 1
        return Copy(sems, number[0] - 1, src, dst, device, sends, receives)

    def both(src, dst_low, dst_high, axis):
        if axis == "t":
            return [copy(src, dst_low, d_tup, t_up, t_dn), copy(src, dst_high, d_tdn, t_dn, t_up)]
        return [copy(src, dst_low, d_rup, r_up, r_dn), copy(src, dst_high, d_rdn, r_dn, r_up)]

    def slot(first, n, piece):
        return kvg.at[pl.ds(first, n), piece]

    out_c0 = copy(slot(4, 2, 0), slot(4, 2, 1), outd, has_out, has_out)
    out_c2 = copy(slot(6, 2, 0), slot(6, 2, 1), outd, has_out, has_out)
    near = has_out & jnp.logical_not(middle)
    out_c1, via_c1, hop_c1 = (copy(slot(2, 2, 0), slot(2, 2, 1), outd, near, near),
                              copy(slot(2, 2, 0), rbuf.at[pl.ds(2, 2)], via, middle, edge),
                              copy(rbuf.at[pl.ds(2, 2)], slot(2, 2, 1), hop, edge, middle))
    out_c4, via_c4, hop_c4 = (copy(slot(0, 2, 0), slot(0, 2, 1), outd, near, near),
                              copy(slot(0, 2, 0), rbuf.at[pl.ds(0, 2)], via, middle, edge),
                              copy(rbuf.at[pl.ds(0, 2)], slot(0, 2, 1), hop, edge, middle))
    mate_kv = copy(slot(0, 8, 0), slot(0, 8, 2), mate)
    rows_pair = copy(slot(8, 4, 0), slot(8, 4, 1), pair)
    rows_far = copy(slot(8, 4, 1), slot(8, 4, 2), fard, far_send, has_far)
    own_pair = copy(slot(4, 2, 0), slot(12, 2, 0), pair)
    own_far = copy(slot(12, 2, 0), slot(14, 2, 0), fard, far_send, has_far)
    out_pair = copy(slot(4, 2, 1), slot(12, 2, 1), pair, has_out, has_out)
    out_far = copy(slot(12, 2, 1), slot(14, 2, 1), fard, far_send & has_out, has_far & has_out)
    mate_pair = copy(slot(12, 2, 0), slot(12, 2, 2), mate)
    mate_far = copy(slot(14, 2, 0), slot(14, 2, 2), mate, has_far, has_far)
    q_row = both(q_all.at[0, pl.ds(2, 2)], q_all.at[1, pl.ds(2, 2)], q_all.at[2, pl.ds(2, 2)], "r")
    q_time = both(q_all.at[0, pl.ds(4, 6)], q_all.at[1, pl.ds(4, 6)], q_all.at[2, pl.ds(4, 6)], "t")
    gi = y * 8 + z
    g_z = [copy(tg.at[gi], tg.at[gi], device) for _, device in peers["z"]]
    g_y = [copy(tg.at[pl.ds(y * 8, 8)], tg.at[pl.ds(y * 8, 8)], device) for _, device in peers["y"]]
    g_x = [copy(tx.at[:, c, x], tx.at[:, c, x], device) for _, device in peers["x"]]
    g_c = copy(tx.at[:, c], tx.at[:, c], mate)
    s_c = [copy(tpo.at[pl.ds(6 * (1 - c), 6)], rco, mate), copy(tpl.at[1 - c], rcl, mate)]
    s_x = [copy(tao.at[:, :, x2], rxo.at[i], device) for i, (x2, device) in enumerate(peers["x"])]
    s_x += [copy(tal.at[:, x2], rxl.at[i], device) for i, (x2, device) in enumerate(peers["x"])]
    s_y = [copy(tb.at[:, :, :, pl.ds(8 * y2, 8)], ry.at[i], device) for i, (y2, device) in enumerate(peers["y"])]
    s_z = [copy(td.at[z2], rz.at[i], device) for i, (z2, device) in enumerate(peers["z"])]
    s_e = copy(te.at[pl.ds(8 * (1 - c), 8)], tr, mate)

    def start(*items):
        for item in items:
            item.start()

    def got(*items):
        for item in items:
            item.wait_recv()

    def norm(value, gain):
        u = value.astype(F32)
        return u * lax.rsqrt(jnp.mean(u * u, axis=-1, keepdims=True) + EPS) * gain[...]

    for h in range(HEADS):
        here = pl.ds(h * D, D)
        raw_t[h] = jnp.broadcast_to(norm(tq[:, here], qg), (8, D))
        raw_t[HEADS + h] = jnp.broadcast_to(norm(tk[:, here], kg), (8, D))
        raw_t[2 * HEADS + h] = jnp.broadcast_to(tv[:, here].astype(F32), (8, D))
    for k, ref in enumerate((vk, vv, vq)):
        for h in range(HEADS):
            raw[k, h] = ref[0, 0, :, pl.ds(h * D, D)]

    def prepare_q(first, n):
        def one(p, _):
            q_all[0, p] = norm(raw[2, order[p]], qg).astype(BF16)
            return 0
        lax.fori_loop(first, first + n, one, 0)

    def prepare_kv(first, n):
        def one(p, _):
            kvg[p, 0, 0] = norm(raw[0, order[p]], kg).astype(BF16)
            kvg[p, 0, 1] = raw[1, order[p]]
            return 0
        lax.fori_loop(first, first + n, one, 0)

    def prepare_text(p, _):
        h = order[p]
        for k in range(3):
            rows[pl.ds(k * HEADS + p, 1), :] = raw_t[k * HEADS + h][:1]
        return 0

    rows[...] = jnp.zeros_like(rows)
    lax.fori_loop(0, HEADS, prepare_text, 0)
    tg[gi] = rows[...].astype(BF16)
    prepare_kv(4, 2)

    count = 14 + has_out.astype(jnp.int32) + t_up.astype(jnp.int32) + t_dn.astype(jnp.int32)
    count = count + r_up.astype(jnp.int32) + r_dn.astype(jnp.int32) + (middle | edge).astype(jnp.int32)
    pl.semaphore_wait(bar, count)

    start(*g_z, out_c0, own_pair)
    prepare_q(4, 6)
    start(*q_time)
    prepare_kv(8, 4)
    start(rows_pair)
    prepare_kv(2, 2)
    start(out_c1, via_c1)
    prepare_kv(6, 2)
    start(out_c2)
    prepare_q(2, 2)
    start(*q_row)
    prepare_kv(0, 2)
    start(out_c4, via_c4, mate_kv)
    prepare_q(0, 2)
    prepare_q(10, 2)

    @pl.when(jnp.logical_not(has_out))
    def _():
        def clear(i, _):
            kvg[jnp.where(i < 8, i, i + 4), 1] = jnp.zeros((2, TOK, D), BF16)
            return 0
        lax.fori_loop(0, 12, clear, 0)

    @pl.when(jnp.logical_not(has_far))
    def _():
        def clear(i, _):
            kvg[8 + i, 2] = jnp.zeros((2, TOK, D), BF16)
            return 0
        lax.fori_loop(0, 4, clear, 0)

    got(*g_z)
    start(*g_y)
    got(rows_pair)
    start(rows_far)

    pen_out = jnp.where(has_out, 0.0, BIG).astype(F32)
    pen_far = jnp.where(has_far, 0.0, BIG).astype(F32)
    index = lax.broadcasted_iota(jnp.int32, (1, TEXT), 1)
    i_c, i_x, i_y, i_z = index // 128, (index // 32) % 4, (index // 8) % 4, index % 8
    original = (i_z % 4) * 64 + i_x * 16 + i_y * 4 + (i_z // 4) * 2 + i_c
    text_bias = jnp.where(original < tlen[0], 0.0, -BIG).astype(F32)
    lane = lax.broadcasted_iota(jnp.int32, (1, D), 1) // 16

    def packed(l, h, old):
        return jnp.where(lane == h, l, old)

    def unpacked(l, h):
        return jnp.sum(jnp.where((lane == h) & (lax.broadcasted_iota(jnp.int32, (1, D), 1) % 16 == 0), l, 0.0),
                       axis=-1, keepdims=True)

    def text(j):
        return tx[j].reshape(TEXT, D)

    def sort_text():
        def widen(i, _):
            tf[pl.ds(pl.multiple_of(i * 8 * TROWS, 8 * TROWS), 8 * TROWS)] = (
                tg[pl.ds(i * 8, 8)].astype(F32).reshape(8 * TROWS, D))
            return 0
        lax.fori_loop(0, 4, widen, 0)

        def pick(j, _):
            tx[j, c, x] = tf[pl.ds(j, 32, stride=TROWS), :].astype(BF16)
            return 0
        lax.fori_loop(0, 3 * HEADS, pick, 0)

    def text_partial():
        for half in range(2):
            def partial(i, l_packed):
                h = half * 6 + i
                o, l = attend(text(h), [(kvg[h, 0, 0], kvg[h, 0, 1], None, None)])
                tpo[h] = o.astype(BF16).reshape(2, 4, 32, D)
                return packed(l, i, l_packed)
            tpl[half] = lax.fori_loop(0, 6, partial, jnp.zeros((TEXT, D), F32)).reshape(2, 4, 32, D)

        @pl.when((t == 0) & (s == 0))
        def _():
            for half in range(2):
                def self_part(i, _):
                    h = half * 6 + i
                    o, l = attend(text(h), [(text(HEADS + h), text(2 * HEADS + h), None, text_bias)])
                    l_packed = tpl[half].reshape(TEXT, D)
                    o, l = merge(tpo[h].reshape(TEXT, D).astype(F32), unpacked(l_packed, i), o, l)
                    tpo[h] = o.astype(BF16).reshape(2, 4, 32, D)
                    tpl[half] = packed(l, i, l_packed).reshape(2, 4, 32, D)
                    return 0
                lax.fori_loop(0, 6, self_part, 0)

    def reduce_c():
        def one(h, l_packed):
            o, l = merge(tpo[6 * c + h].reshape(TEXT, D).astype(F32), unpacked(tpl[c].reshape(TEXT, D), h),
                         rco[h].reshape(TEXT, D).astype(F32), unpacked(rcl[...].reshape(TEXT, D), h))
            tao[h] = o.astype(BF16).reshape(2, 4, 32, D)
            return packed(l, h, l_packed)
        tal[...] = lax.fori_loop(0, 6, one, jnp.zeros((TEXT, D), F32)).reshape(2, 4, 32, D)

    def reduce_x():
        def one(h, _):
            o, l = tao[h, :, x].reshape(64, D).astype(F32), unpacked(tal[:, x].reshape(64, D), h)
            for i in range(3):
                o, l = merge(o, l, rxo[i, h].reshape(64, D).astype(F32), unpacked(rxl[i].reshape(64, D), h))
            tb[h, 0] = o.reshape(2, 32, D)
            tb[h, 1] = jnp.broadcast_to(l, (64, D)).reshape(2, 32, D)
            return 0
        lax.fori_loop(0, 6, one, 0)

    def reduce_y():
        for h in range(6):
            for cc in range(2):
                eight = pl.ds(pl.multiple_of(8 * y, 8), 8)
                o, l = tb[h, 0, cc, eight], tb[h, 1, cc, eight]
                for i in range(3):
                    o, l = merge(o, l, ry[i, h, 0, cc], ry[i, h, 1, cc])
                for k, value in enumerate((o, l)):
                    for zz in range(8):
                        td[zz, pl.ds(k * 16 + cc * 8 + h, 1), :] = value[zz:zz + 1]

    def reduce_z():
        o, l = td[z, pl.ds(0, 16)], td[z, pl.ds(16, 16)]
        for i in range(7):
            o, l = merge(o, l, rz[i, pl.ds(0, 16)], rz[i, pl.ds(16, 16)])
        te[...] = o

    def spread_out(l):
        return jnp.transpose(jnp.broadcast_to(l, (D, TOK)))

    def return_copies(h, d):
        row = h < 4
        dev_t = jnp.where(row, t, t - 1 + 2 * d)
        dev_s = jnp.where(row, s + (2 * d - 1) * SW, s)
        device = (dev_t, dev_s)
        return [
            pltpu.make_async_remote_copy(src_ref=o_send.at[d, h - 2], dst_ref=o_got.at[1 - d, h - 2],
                                         send_sem=ret_s.at[0, d, h - 2], recv_sem=ret_r.at[0, 1 - d, h - 2],
                                         device_id=device, device_id_type=MESH),
            pltpu.make_async_remote_copy(src_ref=l_send.at[d, h - 2], dst_ref=l_got.at[1 - d, h - 2],
                                         send_sem=ret_s.at[1, d, h - 2], recv_sem=ret_r.at[1, 1 - d, h - 2],
                                         device_id=device, device_id_type=MESH),
        ]

    def there(h, d):
        row = h < 4
        low = jnp.where(row, a, t) > 0
        high = jnp.where(row, a - 4, t) < 3
        return (h >= 2) & (h < 10) & jnp.where(d == 0, low, high)

    events = {
        0: lambda: (got(*g_y), sort_text(), start(*g_x), got(rows_far, *q_time)),
        1: lambda: (got(own_pair), start(own_far, mate_pair), got(via_c1), start(hop_c1)),
        2: lambda: (got(out_c0), start(out_pair)),
        3: lambda: (got(*g_x), start(g_c), got(own_far), start(mate_far), got(via_c4), start(hop_c4)),
        4: lambda: (got(g_c), text_partial(), start(*s_c), got(mate_kv, out_c1, hop_c1, *q_row)),
        5: lambda: (got(out_pair), start(out_far), got(*s_c), reduce_c(), start(*s_x)),
        6: lambda: (got(out_c2),),
        8: lambda: (got(*s_x), reduce_x(), start(*s_y), got(out_far, mate_pair, mate_far)),
        9: lambda: (got(*s_y), reduce_y(), start(*s_z)),
        10: lambda: (got(*s_z), reduce_z(), start(s_e), got(out_c4, hop_c4)),
    }

    def step(n, _):
        duo = n // 2
        first = jnp.where(duo == 0, 8, jnp.where(duo == 1, 10, jnp.where(duo == 2, 2, jnp.where(
            duo == 3, 6, jnp.where(duo == 4, 4, 0)))))
        h = first + n % 2
        for at, event in events.items():
            pl.when(n == at)(functools.partial(lambda event: event() and None, event))
        pen_a = jnp.where(h < 8, pen_out, 0.0)
        pen_b = jnp.where(h < 8, 0.0, pen_far)
        relayed = duo == 4

        def one_query(qd, _):
            @pl.when((qd == 0) | there(h, qd - 1))
            def _():
                q = q_all[qd, h]

                def one_group(g, _):
                    group = h + jnp.where(g == 0, 0, 6 + 2 * g)

                    @pl.when((g < 2) | has_far)
                    def _():
                        o, l = attend(q, [
                            (kvg[group, 0, 0], kvg[group, 0, 1], None, None),
                            (kvg[group, 1, 0], kvg[group, 1, 1], pen_a, None),
                            (kvg[group, 2, 0], kvg[group, 2, 1], pen_b, None),
                        ])

                        @pl.when(g == 0)
                        def _():
                            o_own[qd, h] = o
                            l_own[qd, h] = l

                        @pl.when(g > 0)
                        def _():
                            o2, l2 = merge(o_own[qd, h], l_own[qd, h], o, l)
                            o_own[qd, h] = o2
                            l_own[qd, h] = l2
                    return 0

                lax.fori_loop(0, jnp.where(relayed, 3, 1), one_group, 0)

                @pl.when(qd > 0)
                def _():
                    d = qd - 1
                    o_send[d, h - 2] = o_own[qd, h].astype(BF16)
                    l_send[d, h - 2] = jnp.transpose(l_own[qd, h])[:8]
                    for item in return_copies(h, d):
                        item.start()
            return 0

        lax.fori_loop(0, jnp.where((h >= 2) & (h < 10), 3, 1), one_query, 0)
        return 0

    lax.fori_loop(0, 12, step, 0)

    def finish(n, _):
        duo = n // 2
        first = jnp.where(duo == 0, 0, jnp.where(duo == 1, 10, jnp.where(duo == 2, 8, jnp.where(
            duo == 3, 2, jnp.where(duo == 4, 6, 4)))))
        h = first + n % 2
        o, l = attend(q_all[0, h], [(text(HEADS + h), text(2 * HEADS + h), None, text_bias)])
        o, l = merge(o_own[0, h], l_own[0, h], o, l)
        o_own[0, h] = o
        l_own[0, h] = l
        for d in range(2):
            @pl.when(there(h, d))
            def _():
                for item in return_copies(h, 1 - d):
                    item.wait_recv()
                o2, l2 = merge(o_own[0, h], l_own[0, h], o_got[d, h - 2].astype(F32),
                               spread_out(l_got[d, h - 2][:1]))
                o_own[0, h] = o2
                l_own[0, h] = l2
                for item in return_copies(h, d):
                    item.wait_send()
        final[h] = o_own[0, h].astype(BF16)
        return 0

    lax.fori_loop(0, 12, finish, 0)

    got(s_e)
    mine = te[pl.ds(pl.multiple_of(8 * c, 8), 8), :]
    for i in range(6):
        ends[6 * c + i] = jnp.broadcast_to(mine[i:i + 1], (8, D))
        ends[6 * (1 - c) + i] = jnp.broadcast_to(tr[i:i + 1, :], (8, D))
    for h in range(HEADS):
        p = place[h]
        here = pl.ds(h * D, D)
        v_out[0, 0, :, here] = final[p]
        t_out[:, here] = ends[p][:1].astype(BF16)
    for item in ([out_c0, out_c1, out_c2, out_c4, via_c1, via_c4, hop_c1, hop_c4, mate_kv, rows_pair, rows_far, own_pair,
                  own_far, out_pair, out_far, mate_pair, mate_far, g_c, s_e]
                 + q_row + q_time + g_z + g_y + g_x + s_c + s_x + s_y + s_z):
        item.wait_send()


N_COPIES = 64


def main_call(order, place, text_len, arrays):
    shapes = [
        pltpu.VMEM((3, HEADS, TOK, D), BF16),
        pltpu.VMEM((16, 3, 2, TOK, D), BF16),
        pltpu.VMEM((4, 2, TOK, D), BF16),
        pltpu.VMEM((3, HEADS, TOK, D), F32),
        pltpu.VMEM((3, HEADS, TOK, D), F32),
        pltpu.VMEM((2, 8, TOK, D), BF16),
        pltpu.VMEM((2, 8, 8, TOK), F32),
        pltpu.VMEM((2, 8, TOK, D), BF16),
        pltpu.VMEM((2, 8, 8, TOK), F32),
        pltpu.VMEM((HEADS, TOK, D), BF16),
        pltpu.VMEM((3, HEADS, TOK, D), BF16),
        pltpu.VMEM((3 * HEADS, 8, D), F32),
        pltpu.VMEM((TROWS, D), F32),
        pltpu.VMEM((32, TROWS, D), BF16),
        pltpu.VMEM((32 * TROWS, D), F32),
        pltpu.VMEM((3 * HEADS, 2, 4, 32, D), BF16),
        pltpu.VMEM((HEADS, 2, 4, 32, D), BF16),
        pltpu.VMEM((2, 2, 4, 32, D), F32),
        pltpu.VMEM((6, 2, 4, 32, D), BF16),
        pltpu.VMEM((2, 4, 32, D), F32),
        pltpu.VMEM((6, 2, 2, 32, D), F32),
        pltpu.VMEM((8, 32, D), F32),
        pltpu.VMEM((16, D), F32),
        pltpu.VMEM((6, 2, 4, 32, D), BF16),
        pltpu.VMEM((2, 4, 32, D), F32),
        pltpu.VMEM((3, 6, 2, 32, D), BF16),
        pltpu.VMEM((3, 2, 32, D), F32),
        pltpu.VMEM((3, 6, 2, 2, 8, D), F32),
        pltpu.VMEM((7, 32, D), F32),
        pltpu.VMEM((8, D), F32),
        pltpu.VMEM((HEADS, 8, D), F32),
        pltpu.SemaphoreType.DMA((N_COPIES,)),
        pltpu.SemaphoreType.DMA((N_COPIES,)),
        pltpu.SemaphoreType.DMA((2, 2, 8)),
        pltpu.SemaphoreType.DMA((2, 2, 8)),
    ]
    scalars, vmem = pl.BlockSpec(memory_space=pltpu.SMEM), pl.BlockSpec(memory_space=pltpu.VMEM)
    return pl.pallas_call(
        main_kernel,
        out_shape=(jax.ShapeDtypeStruct(arrays[0].shape, BF16), jax.ShapeDtypeStruct(arrays[3].shape, BF16)),
        in_specs=[scalars] * 3 + [vmem] * 8,
        out_specs=(vmem, vmem),
        scratch_shapes=shapes,
        compiler_params=pltpu.CompilerParams(
            collective_id=0, has_side_effects=True, vmem_limit_bytes=VMEM_LIMIT),
        name="tiles",
    )(order, place, text_len, *arrays)


def local(video_q, video_k, video_v, text_q, text_k, text_v, q_gain, k_gain, text_len, window):
    wide = (window == 3).astype(jnp.int32)
    code = wide[:, 0] * 4 + wide[:, 1] * 2 + wide[:, 2]
    rank = jnp.zeros_like(code)
    for value, place in enumerate(RANK_OF_CODE):
        rank = jnp.where(code == value, place, rank)
    key = rank * HEADS + jnp.arange(HEADS, dtype=jnp.int32)
    position = jnp.sum((key[None, :] < key[:, None]).astype(jnp.int32), axis=1)
    places = jnp.arange(HEADS, dtype=jnp.int32)
    order = jnp.sum(jnp.where(position[None, :] == places[:, None], places[None, :], 0), axis=1)

    return main_call(order, position, text_len, (
        video_q, video_k, video_v, text_q, text_k, text_v, q_gain[None], k_gain[None]))


def solution(mesh):
    tiles, rows = P("ta", "sa", None, None), P(("ta", "sa"), None)
    return jax.shard_map(
        local, mesh=mesh,
        in_specs=(tiles, tiles, tiles, rows, rows, rows, P(), P(), P(), P()),
        out_specs=(tiles, rows),
        check_vma=False,
    )
```

time: 195 us -> 156 us (0.80)
  Pallas kernels: 192 us -> 150 us
  local copies, waits for them, and re-layouts: 0 us -> 2.97 us
    pallas_call x3 -> x1, Pallas kernels: 192 us -> 150 us  [main_call(): pl.pallas_call(main_kernel, out_shape=(jax.ShapeDtypeStruct(arrays[0].sha...]
    unnamed x0 -> x6, local copies, waits for them, and re-layouts: none -> 2.97 us
where the time goes in v2:
time: 156 us; the launch traced here: 155 us
  Pallas kernels  150 us (96%)
  local copies, waits for them, and re-layouts  2.97 us (2%)
    pallas_call x1, Pallas kernels, main_call(): pl.pallas_call(main_kernel, out_shape=(jax.ShapeDtypeStruct(arrays[0].sha...  150 us

profile of v2, /device:TPU:36, one launch (start us, length us, event | category | flops | bytes accessed | tf_op | source)
XLA Modules:
  0.0 155.3 jit_solution(2025674063659468870)
XLA Ops:
  1.3 0.7 compare_convert_fusion
  2.0 0.2 convert_reduce_fusion.place
  2.2 0.0 copy-start.1
  2.2 0.6 select_reduce_fusion.order
  2.8 0.0 copy-done.1
  2.8 149.5 %tiles.1 = (bf16[1,1,384,1536]{3,2,1,0:T(8,128)(2,1)}, bf16[1,1536]{1,0:T(2,128)(2,1)}) custom-call(s32[12]{0:T(128)} %select_reduce_fusion.order, s32[12]{0:T(128)} %copy-done.1, s32[1]{0:T(128)S(6)} %copy.14.tlen, bf16[1,1,384,1536]{3,2,1,0:T(8,128)(2,1)} %vq.1, bf16[1,1,384,1536]{3,2,1,0:T(8,128)(2,1)} %vk.1, bf16[1,1,384,1536]{3,2,1,0:T(8,128)(2,1)} %vv.1, ...), custom_call_target="tpu_custom_call" | custom-call | tf_op jit(solution)/shard_map/tiles/pallas_call | solution.py:526
  152.3 0.0 copy-start
  152.3 2.4 %copy.15 = bf16[1,1,384,1536]{3,2,1,0:T(8,128)(2,1)} copy(bf16[1,1,384,1536]{3,2,1,0:T(8,128)(2,1)} %get-tuple-element.6) | data formatting | bytes 2359296
  154.7 0.0 copy-done
  154.7 0.6 copy.16
  (2 shorter events, 0.0 us)
Async XLA Ops:
  2.2 0.6 copy-start.1
  152.3 2.4 %copy-start = (bf16[1,1536]{1,0:T(2,128)(2,1)S(1)}, bf16[1,1536]{1,0:T(2,128)(2,1)}, u32[]{:S(2)}) copy-start(bf16[1,1536]{1,0:T(2,128)(2,1)} %get-tuple-element.7) | copy-start | bytes 9220

commit v3 on v2

--- a/solution.py
+++ b/solution.py
@@ -31,28 +31,48 @@
     return lax.dot_general(a, b, (((1,), (1,)), ((), ())), preferred_element_type=F32)
 
 
-def attend(q, pieces):
+def attend(q, pieces, bias=None):
     cc = math.log2(math.e) / math.sqrt(D)
     scores, peak = [], None
-    for k, v, penalty, bias in pieces:
+    for k, v in pieces:
         s = dot_t(q, k)
         if bias is not None:
             s = s + bias
         scores.append(s)
         row = jnp.max(s, axis=-1, keepdims=True)
-        if penalty is not None:
-            row = row - penalty
         peak = row if peak is None else jnp.maximum(peak, row)
     peak = peak * cc
     total = None
-    for s, (k, v, penalty, bias) in zip(scores, pieces):
-        shift = peak if penalty is None else peak + penalty
-        w = jnp.exp2(s * cc - shift).astype(BF16)
-        ones = jnp.ones(v.shape, BF16)
-        part = jnp.dot(w, jnp.concatenate([v, ones], axis=1), preferred_element_type=F32)
+    for s, (k, v) in zip(scores, pieces):
+        w = jnp.exp2(s * cc - peak).astype(BF16)
+        part = jnp.dot(w, jnp.concatenate([v, jnp.ones(v.shape, BF16)], axis=1), preferred_element_type=F32)
         total = part if total is None else total + part
     o, l = total[:, :D], total[:, D:]
     return o / l, peak + jnp.log2(l)
+
+
+def absorb(q, pieces, state, bias=None):
+    cc = math.log2(math.e) / math.sqrt(D)
+    acc, l, m = state
+    scores, peak = [], None
+    for k, v in pieces:
+        s = dot_t(q, k)
+        if bias is not None:
+            s = s + bias
+        scores.append(s)
+        for i in range(0, s.shape[1], D):
+            part = s[:, i:i + D]
+            peak = part if peak is None else jnp.maximum(peak, part)
+    new = jnp.maximum(m, jnp.max(peak, axis=-1, keepdims=True) * cc)
+    scale = jnp.exp2(m - new)
+    shift = new[:, :1]
+    acc, l = acc * scale, l * scale
+    for s, (k, v) in zip(scores, pieces):
+        w = jnp.exp2(s * cc - shift)
+        for i in range(0, s.shape[1], D):
+            l = l + w[:, i:i + D]
+        acc = acc + jnp.dot(w.astype(BF16), v, preferred_element_type=F32)
+    return acc, l, new
 
 
 class Copy:
@@ -80,7 +100,7 @@
 
 
 def main_kernel(order, place, tlen, vq, vk, vv, tq, tk, tv, qg, kg, v_out, t_out,
-                q_all, kvg, rbuf, o_own, l_own, o_send, l_send, o_got, l_got, final,
+                q_all, kvg, rbuf, acc, tot, top, o_send, l_send, o_got, l_got, final,
                 raw, raw_t, rows, tg, tf, tx, tpo, tpl, tao, tal, tb, td, te, rco, rcl, rxo, rxl, ry, rz, tr, ends,
                 ssem, rsem, ret_s, ret_r):
     t = lax.axis_index("ta")
@@ -146,31 +166,34 @@
     def slot(first, n, piece):
         return kvg.at[pl.ds(first, n), piece]
 
-    out_c0 = copy(slot(4, 2, 0), slot(4, 2, 1), outd, has_out, has_out)
-    out_c2 = copy(slot(6, 2, 0), slot(6, 2, 1), outd, has_out, has_out)
+    out_c0 = copy(slot(4, 2, 0), slot(4, 2, 2), outd, has_out, has_out)
+    out_c2 = copy(slot(6, 2, 0), slot(6, 2, 2), outd, has_out, has_out)
     near = has_out & jnp.logical_not(middle)
-    out_c1, via_c1, hop_c1 = (copy(slot(2, 2, 0), slot(2, 2, 1), outd, near, near),
+    out_c1, via_c1, hop_c1 = (copy(slot(2, 2, 0), slot(2, 2, 2), outd, near, near),
                               copy(slot(2, 2, 0), rbuf.at[pl.ds(2, 2)], via, middle, edge),
-                              copy(rbuf.at[pl.ds(2, 2)], slot(2, 2, 1), hop, edge, middle))
-    out_c4, via_c4, hop_c4 = (copy(slot(0, 2, 0), slot(0, 2, 1), outd, near, near),
+                              copy(rbuf.at[pl.ds(2, 2)], slot(2, 2, 2), hop, edge, middle))
+    out_c4, via_c4, hop_c4 = (copy(slot(0, 2, 0), slot(0, 2, 2), outd, near, near),
                               copy(slot(0, 2, 0), rbuf.at[pl.ds(0, 2)], via, middle, edge),
-                              copy(rbuf.at[pl.ds(0, 2)], slot(0, 2, 1), hop, edge, middle))
-    mate_kv = copy(slot(0, 8, 0), slot(0, 8, 2), mate)
+                              copy(rbuf.at[pl.ds(0, 2)], slot(0, 2, 2), hop, edge, middle))
+    mate_kv = copy(slot(0, 8, 0), slot(0, 8, 1), mate)
     rows_pair = copy(slot(8, 4, 0), slot(8, 4, 1), pair)
     rows_far = copy(slot(8, 4, 1), slot(8, 4, 2), fard, far_send, has_far)
     own_pair = copy(slot(4, 2, 0), slot(12, 2, 0), pair)
     own_far = copy(slot(12, 2, 0), slot(14, 2, 0), fard, far_send, has_far)
-    out_pair = copy(slot(4, 2, 1), slot(12, 2, 1), pair, has_out, has_out)
-    out_far = copy(slot(12, 2, 1), slot(14, 2, 1), fard, far_send & has_out, has_far & has_out)
-    mate_pair = copy(slot(12, 2, 0), slot(12, 2, 2), mate)
-    mate_far = copy(slot(14, 2, 0), slot(14, 2, 2), mate, has_far, has_far)
+    out_pair = copy(slot(4, 2, 2), slot(12, 2, 2), pair, has_out, has_out)
+    out_far = copy(slot(12, 2, 2), slot(14, 2, 2), fard, far_send & has_out, has_far & has_out)
+    mate_pair = copy(slot(12, 2, 0), slot(12, 2, 1), mate)
+    mate_far = copy(slot(14, 2, 0), slot(14, 2, 1), mate, has_far, has_far)
     q_row = both(q_all.at[0, pl.ds(2, 2)], q_all.at[1, pl.ds(2, 2)], q_all.at[2, pl.ds(2, 2)], "r")
     q_time = both(q_all.at[0, pl.ds(4, 6)], q_all.at[1, pl.ds(4, 6)], q_all.at[2, pl.ds(4, 6)], "t")
     gi = y * 8 + z
     g_z = [copy(tg.at[gi], tg.at[gi], device) for _, device in peers["z"]]
     g_y = [copy(tg.at[pl.ds(y * 8, 8)], tg.at[pl.ds(y * 8, 8)], device) for _, device in peers["y"]]
-    g_x = [copy(tx.at[:, c, x], tx.at[:, c, x], device) for _, device in peers["x"]]
-    g_c = copy(tx.at[:, c], tx.at[:, c], mate)
+    first, rest = pl.ds(0, HEADS), pl.ds(HEADS, 2 * HEADS)
+    g_xq = [copy(tx.at[first, c, x], tx.at[first, c, x], device) for _, device in peers["x"]]
+    g_xkv = [copy(tx.at[rest, c, x], tx.at[rest, c, x], device) for _, device in peers["x"]]
+    g_cq = copy(tx.at[first, c], tx.at[first, c], mate)
+    g_ckv = copy(tx.at[rest, c], tx.at[rest, c], mate)
     s_c = [copy(tpo.at[pl.ds(6 * (1 - c), 6)], rco, mate), copy(tpl.at[1 - c], rcl, mate)]
     s_x = [copy(tao.at[:, :, x2], rxo.at[i], device) for i, (x2, device) in enumerate(peers["x"])]
     s_x += [copy(tal.at[:, x2], rxl.at[i], device) for i, (x2, device) in enumerate(peers["x"])]
@@ -227,43 +250,6 @@
     count = count + r_up.astype(jnp.int32) + r_dn.astype(jnp.int32) + (middle | edge).astype(jnp.int32)
     pl.semaphore_wait(bar, count)
 
-    start(*g_z, out_c0, own_pair)
-    prepare_q(4, 6)
-    start(*q_time)
-    prepare_kv(8, 4)
-    start(rows_pair)
-    prepare_kv(2, 2)
-    start(out_c1, via_c1)
-    prepare_kv(6, 2)
-    start(out_c2)
-    prepare_q(2, 2)
-    start(*q_row)
-    prepare_kv(0, 2)
-    start(out_c4, via_c4, mate_kv)
-    prepare_q(0, 2)
-    prepare_q(10, 2)
-
-    @pl.when(jnp.logical_not(has_out))
-    def _():
-        def clear(i, _):
-            kvg[jnp.where(i < 8, i, i + 4), 1] = jnp.zeros((2, TOK, D), BF16)
-            return 0
-        lax.fori_loop(0, 12, clear, 0)
-
-    @pl.when(jnp.logical_not(has_far))
-    def _():
-        def clear(i, _):
-            kvg[8 + i, 2] = jnp.zeros((2, TOK, D), BF16)
-            return 0
-        lax.fori_loop(0, 4, clear, 0)
-
-    got(*g_z)
-    start(*g_y)
-    got(rows_pair)
-    start(rows_far)
-
-    pen_out = jnp.where(has_out, 0.0, BIG).astype(F32)
-    pen_far = jnp.where(has_far, 0.0, BIG).astype(F32)
     index = lax.broadcasted_iota(jnp.int32, (1, TEXT), 1)
     i_c, i_x, i_y, i_z = index // 128, (index // 32) % 4, (index // 8) % 4, index % 8
     original = (i_z % 4) * 64 + i_x * 16 + i_y * 4 + (i_z // 4) * 2 + i_c
@@ -296,23 +282,10 @@
         for half in range(2):
             def partial(i, l_packed):
                 h = half * 6 + i
-                o, l = attend(text(h), [(kvg[h, 0, 0], kvg[h, 0, 1], None, None)])
+                o, l = attend(text(h), [(kvg[h, 0, 0], kvg[h, 0, 1])])
                 tpo[h] = o.astype(BF16).reshape(2, 4, 32, D)
                 return packed(l, i, l_packed)
             tpl[half] = lax.fori_loop(0, 6, partial, jnp.zeros((TEXT, D), F32)).reshape(2, 4, 32, D)
-
-        @pl.when((t == 0) & (s == 0))
-        def _():
-            for half in range(2):
-                def self_part(i, _):
-                    h = half * 6 + i
-                    o, l = attend(text(h), [(text(HEADS + h), text(2 * HEADS + h), None, text_bias)])
-                    l_packed = tpl[half].reshape(TEXT, D)
-                    o, l = merge(tpo[h].reshape(TEXT, D).astype(F32), unpacked(l_packed, i), o, l)
-                    tpo[h] = o.astype(BF16).reshape(2, 4, 32, D)
-                    tpl[half] = packed(l, i, l_packed).reshape(2, 4, 32, D)
-                    return 0
-                lax.fori_loop(0, 6, self_part, 0)
 
     def reduce_c():
         def one(h, l_packed):
@@ -331,6 +304,17 @@
             tb[h, 1] = jnp.broadcast_to(l, (64, D)).reshape(2, 32, D)
             return 0
         lax.fori_loop(0, 6, one, 0)
+
+        @pl.when((y == 0) & (z == 0))
+        def _():
+            def self_part(h, _):
+                k = 6 * c + h
+                o, l = attend(tx[k, :, x].reshape(64, D), [(text(HEADS + k), text(2 * HEADS + k))], text_bias)
+                o, l = merge(tb[h, 0].reshape(64, D), tb[h, 1].reshape(64, D), o, l)
+                tb[h, 0] = o.reshape(2, 32, D)
+                tb[h, 1] = l.reshape(2, 32, D)
+                return 0
+            lax.fori_loop(0, 6, self_part, 0)
 
     def reduce_y():
         for h in range(6):
@@ -351,6 +335,26 @@
 
     def spread_out(l):
         return jnp.transpose(jnp.broadcast_to(l, (D, TOK)))
+
+    start(*g_z)
+    prepare_q(4, 6)
+    got(*g_z)
+    start(*g_y)
+    prepare_kv(8, 4)
+    prepare_kv(6, 2)
+    got(*g_y)
+    sort_text()
+    start(*g_xq)
+    start(out_c0, own_pair, *q_time)
+    start(rows_pair, out_c2)
+    prepare_kv(2, 2)
+    start(out_c1, via_c1)
+    prepare_kv(0, 2)
+    start(mate_kv, out_c4, via_c4, *g_xkv)
+    prepare_q(2, 2)
+    start(*q_row)
+    prepare_q(0, 2)
+    prepare_q(10, 2)
 
     def return_copies(h, d):
         row = h < 4
@@ -372,98 +376,105 @@
         high = jnp.where(row, a - 4, t) < 3
         return (h >= 2) & (h < 10) & jnp.where(d == 0, low, high)
 
-    events = {
-        0: lambda: (got(*g_y), sort_text(), start(*g_x), got(rows_far, *q_time)),
-        1: lambda: (got(own_pair), start(own_far, mate_pair), got(via_c1), start(hop_c1)),
-        2: lambda: (got(out_c0), start(out_pair)),
-        3: lambda: (got(*g_x), start(g_c), got(own_far), start(mate_far), got(via_c4), start(hop_c4)),
-        4: lambda: (got(g_c), text_partial(), start(*s_c), got(mate_kv, out_c1, hop_c1, *q_row)),
-        5: lambda: (got(out_pair), start(out_far), got(*s_c), reduce_c(), start(*s_x)),
-        6: lambda: (got(out_c2),),
-        8: lambda: (got(*s_x), reduce_x(), start(*s_y), got(out_far, mate_pair, mate_far)),
-        9: lambda: (got(*s_y), reduce_y(), start(*s_z)),
-        10: lambda: (got(*s_z), reduce_z(), start(s_e), got(out_c4, hop_c4)),
-    }
-
-    def step(n, _):
-        duo = n // 2
-        first = jnp.where(duo == 0, 8, jnp.where(duo == 1, 10, jnp.where(duo == 2, 2, jnp.where(
-            duo == 3, 6, jnp.where(duo == 4, 4, 0)))))
-        h = first + n % 2
-        for at, event in events.items():
-            pl.when(n == at)(functools.partial(lambda event: event() and None, event))
-        pen_a = jnp.where(h < 8, pen_out, 0.0)
-        pen_b = jnp.where(h < 8, 0.0, pen_far)
-        relayed = duo == 4
-
-        def one_query(qd, _):
-            @pl.when((qd == 0) | there(h, qd - 1))
+    def reset(i, _):
+        for ref, value in ((acc, 0.0), (tot, 0.0), (top, -BIG)):
+            ref[i // HEADS, i % HEADS] = jnp.full((TOK, D), value, F32)
+        return 0
+
+    lax.fori_loop(0, 3 * HEADS, reset, 0)
+
+    def take(h, n, pieces, bias=None):
+        refs = (acc, tot, top)
+        state = [ref[:n, h].reshape(n * TOK, D) for ref in refs]
+        for ref, value in zip(refs, absorb(q_all[:n, h].reshape(n * TOK, D), pieces, state, bias)):
+            ref[:n, h] = value.reshape(n, TOK, D)
+
+    segments = [
+        (3, 8, 2, 0, 1, lambda: (
+            got(*g_xq), start(g_cq), got(own_pair), start(own_far, mate_pair), got(g_cq), text_partial(), start(*s_c),
+            got(rows_pair), start(rows_far), got(*s_c), reduce_c(), start(*s_x), got(rows_far, *q_time))),
+        (1, 10, 2, 0, 0, lambda: (got(*g_xkv), start(g_ckv), got(own_far), start(mate_far))),
+        (0, 0, 12, 0, 0, lambda: (got(via_c1), start(hop_c1), got(g_ckv), got(*s_x), reduce_x(), start(*s_y))),
+        (3, 4, 2, 0, 0, lambda: (got(out_c0), start(out_pair), got(mate_kv))),
+        (3, 4, 2, 1, 0, lambda: (got(via_c4), start(hop_c4), got(mate_pair, out_pair), start(out_far), got(*s_y), reduce_y(), start(*s_z))),
+        (3, 6, 2, 0, 1, lambda: (got(out_c2),)),
+        (3, 4, 2, 2, 1, lambda: (got(mate_far, out_far), got(*s_z), reduce_z(), start(s_e))),
+        (3, 2, 2, 0, 1, lambda: (got(out_c1, hop_c1, *q_row))),
+        (1, 0, 2, 0, 0, lambda: got(out_c4, hop_c4)),
+    ]
+
+    def pick_of(n, field):
+        value = segments[0][field]
+        for i in range(1, len(segments)):
+            if segments[i][field] != segments[i - 1][field]:
+                value = jnp.where(n >= i, segments[i][field], value)
+        return value
+
+    def segment(n, _):
+        for i, item in enumerate(segments):
+            pl.when(n == i)(functools.partial(lambda event: event() and None, item[5]))
+        kind, h0, nh, g, back = (pick_of(n, field) for field in range(5))
+        present = (g < 2) | has_far
+
+        def work(i, _):
+            h = h0 + i
+            group = h + jnp.where(g == 0, 0, 6 + 2 * g)
+            late = jnp.where(h < 8, has_out, has_far)
+            pieces = [(kvg.at[group, j, 0], kvg.at[group, j, 1]) for j in range(3)]
+
+            def read(count):
+                return [(k[...], v[...]) for k, v in pieces[:count]]
+
+            for n_q in (3, 1):
+                @pl.when((kind == n_q) & present & late)
+                def _():
+                    take(h, n_q, read(3))
+
+                @pl.when((kind == n_q) & present & jnp.logical_not(late))
+                def _():
+                    take(h, n_q, read(2))
+
+            @pl.when(kind == 0)
             def _():
-                q = q_all[qd, h]
-
-                def one_group(g, _):
-                    group = h + jnp.where(g == 0, 0, 6 + 2 * g)
-
-                    @pl.when((g < 2) | has_far)
-                    def _():
-                        o, l = attend(q, [
-                            (kvg[group, 0, 0], kvg[group, 0, 1], None, None),
-                            (kvg[group, 1, 0], kvg[group, 1, 1], pen_a, None),
-                            (kvg[group, 2, 0], kvg[group, 2, 1], pen_b, None),
-                        ])
-
-                        @pl.when(g == 0)
-                        def _():
-                            o_own[qd, h] = o
-                            l_own[qd, h] = l
-
-                        @pl.when(g > 0)
-                        def _():
-                            o2, l2 = merge(o_own[qd, h], l_own[qd, h], o, l)
-                            o_own[qd, h] = o2
-                            l_own[qd, h] = l2
-                    return 0
-
-                lax.fori_loop(0, jnp.where(relayed, 3, 1), one_group, 0)
-
-                @pl.when(qd > 0)
+                take(h, 1, [(text(HEADS + h), text(2 * HEADS + h))], text_bias)
+
+            for d in range(2):
+                @pl.when((back == 1) & there(h, d))
                 def _():
-                    d = qd - 1
-                    o_send[d, h - 2] = o_own[qd, h].astype(BF16)
-                    l_send[d, h - 2] = jnp.transpose(l_own[qd, h])[:8]
+                    total = jnp.sum(tot[d + 1, h], axis=-1, keepdims=True)
+                    o_send[d, h - 2] = (acc[d + 1, h] / total).astype(BF16)
+                    l_send[d, h - 2] = jnp.transpose(top[d + 1, h] + jnp.log2(total))[:8]
                     for item in return_copies(h, d):
                         item.start()
             return 0
 
-        lax.fori_loop(0, jnp.where((h >= 2) & (h < 10), 3, 1), one_query, 0)
+        lax.fori_loop(0, nh, work, 0)
         return 0
 
-    lax.fori_loop(0, 12, step, 0)
+    lax.fori_loop(0, len(segments), segment, 0)
 
     def finish(n, _):
         duo = n // 2
-        first = jnp.where(duo == 0, 0, jnp.where(duo == 1, 10, jnp.where(duo == 2, 8, jnp.where(
-            duo == 3, 2, jnp.where(duo == 4, 6, 4)))))
-        h = first + n % 2
-        o, l = attend(q_all[0, h], [(text(HEADS + h), text(2 * HEADS + h), None, text_bias)])
-        o, l = merge(o_own[0, h], l_own[0, h], o, l)
-        o_own[0, h] = o
-        l_own[0, h] = l
+        h = jnp.where(duo == 0, 0, jnp.where(duo == 1, 10, jnp.where(duo == 2, 8, jnp.where(
+            duo == 3, 6, jnp.where(duo == 4, 4, 2))))) + n % 2
         for d in range(2):
             @pl.when(there(h, d))
             def _():
                 for item in return_copies(h, 1 - d):
                     item.wait_recv()
-                o2, l2 = merge(o_own[0, h], l_own[0, h], o_got[d, h - 2].astype(F32),
-                               spread_out(l_got[d, h - 2][:1]))
-                o_own[0, h] = o2
-                l_own[0, h] = l2
+                theirs = spread_out(l_got[d, h - 2][:1])
+                mine = top[0, h]
+                new = jnp.maximum(mine, theirs)
+                w1, w2 = jnp.exp2(mine - new), jnp.exp2(theirs - new)
+                acc[0, h] = acc[0, h] * w1 + o_got[d, h - 2].astype(F32) * w2
+                tot[0, h] = tot[0, h] * w1 + w2 * (1.0 / D)
+                top[0, h] = new
                 for item in return_copies(h, d):
                     item.wait_send()
-        final[h] = o_own[0, h].astype(BF16)
+        final[h] = (acc[0, h] / jnp.sum(tot[0, h], axis=-1, keepdims=True)).astype(BF16)
         return 0
 
-    lax.fori_loop(0, 12, finish, 0)
+    lax.fori_loop(0, HEADS, finish, 0)
 
     got(s_e)
     mine = te[pl.ds(pl.multiple_of(8 * c, 8), 8), :]
@@ -476,8 +487,8 @@
         v_out[0, 0, :, here] = final[p]
         t_out[:, here] = ends[p][:1].astype(BF16)
     for item in ([out_c0, out_c1, out_c2, out_c4, via_c1, via_c4, hop_c1, hop_c4, mate_kv, rows_pair, rows_far, own_pair,
-                  own_far, out_pair, out_far, mate_pair, mate_far, g_c, s_e]
-                 + q_row + q_time + g_z + g_y + g_x + s_c + s_x + s_y + s_z):
+                  own_far, out_pair, out_far, mate_pair, mate_far, g_cq, g_ckv, s_e]
+                 + q_row + q_time + g_z + g_y + g_xq + g_xkv + s_c + s_x + s_y + s_z):
         item.wait_send()
 
 
@@ -489,6 +500,7 @@
         pltpu.VMEM((3, HEADS, TOK, D), BF16),
         pltpu.VMEM((16, 3, 2, TOK, D), BF16),
         pltpu.VMEM((4, 2, TOK, D), BF16),
+        pltpu.VMEM((3, HEADS, TOK, D), F32),
         pltpu.VMEM((3, HEADS, TOK, D), F32),
         pltpu.VMEM((3, HEADS, TOK, D), F32),
         pltpu.VMEM((2, 8, TOK, D), BF16),

time: 156 us -> 140 us (0.90)
  the two profiles are of different devices: /device:TPU:36 before, /device:TPU:90 now
where the time goes in v3:
time: 140 us
  Pallas kernels  134 us (96%)
  local copies, waits for them, and re-layouts  2.97 us (2%)
  other arithmetic  1.51 us (1%)
    pallas_call x1, Pallas kernels, main_call(): pl.pallas_call(main_kernel, out_shape=(jax.ShapeDtypeStruct(arrays[0].sha...  134 us
    unnamed x6, local copies, waits for them, and re-layouts  2.97 us

profile of v3, /device:TPU:90, one launch (start us, length us, event | category | flops | bytes accessed | tf_op | source)
XLA Modules:
  0.0 140.0 jit_solution(11493099499755326348)
XLA Ops:
  1.3 0.7 compare_convert_fusion
  2.0 0.2 convert_reduce_fusion.place
  2.2 0.0 copy-start.1
  2.2 0.6 select_reduce_fusion.order
  2.8 0.0 copy-done.1
  2.8 134.2 %tiles.1 = (bf16[1,1,384,1536]{3,2,1,0:T(8,128)(2,1)}, bf16[1,1536]{1,0:T(2,128)(2,1)}) custom-call(s32[12]{0:T(128)} %select_reduce_fusion.order, s32[12]{0:T(128)} %copy-done.1, s32[1]{0:T(128)S(6)} %copy.14.tlen, bf16[1,1,384,1536]{3,2,1,0:T(8,128)(2,1)} %vq.1, bf16[1,1,384,1536]{3,2,1,0:T(8,128)(2,1)} %vk.1, bf16[1,1,384,1536]{3,2,1,0:T(8,128)(2,1)} %vv.1, ...), custom_call_target="tpu_custom_call" | custom-call | tf_op jit(solution)/shard_map/tiles/pallas_call | solution.py:538
  137.0 0.0 copy-start
  137.0 2.4 %copy.15 = bf16[1,1,384,1536]{3,2,1,0:T(8,128)(2,1)} copy(bf16[1,1,384,1536]{3,2,1,0:T(8,128)(2,1)} %get-tuple-element.6) | data formatting | bytes 2359296
  139.4 0.0 copy-done
  139.4 0.6 copy.16
  (2 shorter events, 0.0 us)
Async XLA Ops:
  2.2 0.6 copy-start.1
  137.0 2.4 %copy-start = (bf16[1,1536]{1,0:T(2,128)(2,1)S(1)}, bf16[1,1536]{1,0:T(2,128)(2,1)}, u32[]{:S(2)}) copy-start(bf16[1,1536]{1,0:T(2,128)(2,1)} %get-tuple-element.7) | copy-start | bytes 9220

commit v4 on v3

--- a/solution.py
+++ b/solution.py
@@ -394,12 +394,12 @@
             got(*g_xq), start(g_cq), got(own_pair), start(own_far, mate_pair), got(g_cq), text_partial(), start(*s_c),
             got(rows_pair), start(rows_far), got(*s_c), reduce_c(), start(*s_x), got(rows_far, *q_time))),
         (1, 10, 2, 0, 0, lambda: (got(*g_xkv), start(g_ckv), got(own_far), start(mate_far))),
-        (0, 0, 12, 0, 0, lambda: (got(via_c1), start(hop_c1), got(g_ckv), got(*s_x), reduce_x(), start(*s_y))),
-        (3, 4, 2, 0, 0, lambda: (got(out_c0), start(out_pair), got(mate_kv))),
+        (3, 4, 2, 0, 0, lambda: (got(out_c0), start(out_pair), got(mate_kv), got(via_c1), start(hop_c1))),
+        (0, 0, 12, 0, 0, lambda: (got(g_ckv), got(*s_x), reduce_x(), start(*s_y))),
         (3, 4, 2, 1, 0, lambda: (got(via_c4), start(hop_c4), got(mate_pair, out_pair), start(out_far), got(*s_y), reduce_y(), start(*s_z))),
         (3, 6, 2, 0, 1, lambda: (got(out_c2),)),
+        (3, 2, 2, 0, 1, lambda: (got(out_c1, hop_c1, *q_row))),
         (3, 4, 2, 2, 1, lambda: (got(mate_far, out_far), got(*s_z), reduce_z(), start(s_e))),
-        (3, 2, 2, 0, 1, lambda: (got(out_c1, hop_c1, *q_row))),
         (1, 0, 2, 0, 0, lambda: got(out_c4, hop_c4)),
     ]
 
@@ -456,7 +456,7 @@
     def finish(n, _):
         duo = n // 2
         h = jnp.where(duo == 0, 0, jnp.where(duo == 1, 10, jnp.where(duo == 2, 8, jnp.where(
-            duo == 3, 6, jnp.where(duo == 4, 4, 2))))) + n % 2
+            duo == 3, 6, jnp.where(duo == 4, 2, 4))))) + n % 2
         for d in range(2):
             @pl.when(there(h, d))
             def _():

time: 140 us -> 133 us (0.950)
  the two profiles are of different devices: /device:TPU:90 before, /device:TPU:154 now
where the time goes in v4:
time: 133 us
  Pallas kernels  127 us (95%)
  local copies, waits for them, and re-layouts  2.97 us (2%)
  other arithmetic  1.51 us (1%)
    pallas_call x1, Pallas kernels, main_call(): pl.pallas_call(main_kernel, out_shape=(jax.ShapeDtypeStruct(arrays[0].sha...  127 us
    unnamed x6, local copies, waits for them, and re-layouts  2.97 us

profile of v4, /device:TPU:154, one launch (start us, length us, event | category | flops | bytes accessed | tf_op | source)
XLA Modules:
  0.0 133.2 jit_solution(15430339064728907149)
XLA Ops:
  1.3 0.7 compare_convert_fusion
  2.0 0.2 convert_reduce_fusion.place
  2.2 0.0 copy-start.1
  2.2 0.6 select_reduce_fusion.order
  2.8 0.0 copy-done.1
  2.8 127.4 %tiles.1 = (bf16[1,1,384,1536]{3,2,1,0:T(8,128)(2,1)}, bf16[1,1536]{1,0:T(2,128)(2,1)}) custom-call(s32[12]{0:T(128)} %select_reduce_fusion.order, s32[12]{0:T(128)} %copy-done.1, s32[1]{0:T(128)S(6)} %copy.14.tlen, bf16[1,1,384,1536]{3,2,1,0:T(8,128)(2,1)} %vq.1, bf16[1,1,384,1536]{3,2,1,0:T(8,128)(2,1)} %vk.1, bf16[1,1,384,1536]{3,2,1,0:T(8,128)(2,1)} %vv.1, ...), custom_call_target="tpu_custom_call" | custom-call | tf_op jit(solution)/shard_map/tiles/pallas_call | solution.py:538
  130.2 0.0 copy-start
  130.2 2.4 %copy.15 = bf16[1,1,384,1536]{3,2,1,0:T(8,128)(2,1)} copy(bf16[1,1,384,1536]{3,2,1,0:T(8,128)(2,1)} %get-tuple-element.6) | data formatting | bytes 2359296
  132.6 0.0 copy-done
  132.6 0.6 copy.16
  (2 shorter events, 0.0 us)
Async XLA Ops:
  2.2 0.6 copy-start.1
  130.2 2.4 %copy-start = (bf16[1,1536]{1,0:T(2,128)(2,1)S(1)}, bf16[1,1536]{1,0:T(2,128)(2,1)}, u32[]{:S(2)}) copy-start(bf16[1,1536]{1,0:T(2,128)(2,1)} %get-tuple-element.7) | copy-start | bytes 9220
